TPU v7x, 32 devices: a whole 2x2x4 slice. The times are simulated.
32 devices in a mesh: qry: 8 (over z, core), lib: 4 (over y, x).
Axes of the slice: x: 2, y: 2, z: 4, core: 2. Of those that a mesh axis runs over, the one named last changes fastest.
Arguments:
- query_prints: bfloat16 [256, 2048], P('qry'), may hold values from -500 to 500, as said below
- library_prints: bfloat16 [24576, 2048], P(('lib', 'qry')), may hold values from -1500 to 1500
- query_atoms: float32 [256, 192], P(('qry', 'lib')), may hold values from -3 to 3, as said below
- conformer_atoms: float32 [24576, 192], P(('lib', 'qry')), may hold values from -3 to 3, as said below
- candidates: int32 [256, 64], P(('qry', 'lib')), may hold values from 0 to 24575, as said below
- candidate_count: int32 [256], P(('qry', 'lib')), may hold values from 16 to 64
- home_row: int32 [24576], replicated, may hold values from 0 to 24575, as said below
Outputs:
- tversky: bfloat16 [256, 24576], P(None, ('lib', 'qry'))
- rescore: float32 [256, 64], P(('qry', 'lib'))
Inputs may be any that keep to these rules, and one draw needn't show every extreme that they name: query_prints rows and columns carry independent positive scales. `query_atoms`: each row holds x, y and z of 48 atom slots, then their weights; a padded slot has weight 0, and every row has at least one atom of positive weight. `conformer_atoms`: each row holds x, y and z of 48 atom slots, then their weights; a padded slot has weight 0, and every row has at least one atom of positive weight. Among the candidates in the rows of one device (8 queries, padding included), at most 36 have storage rows in any one block of rows b * 768 to (b + 1) * 768 - 1; in every draw some such block receives exactly 36 from the rows of every device. `home_row`: a permutation of 0 to 24575.
All inputs are finite; a program needn't handle non-finite values.
Results may differ from a plain program's by a relative error of at most 0.0029.
Values may be sent and summed in bfloat16 or wider, within the bound.
A program may use at most 64 MiB of HBM per device.

v0:
```python
import functools
import math

import jax
import jax.numpy as jnp
from jax import lax
from jax.experimental import pallas as pl
from jax.experimental.pallas import tpu as pltpu
from jax.sharding import PartitionSpec as P

SHARPNESS = 0.8
EPSILON = 1e-06
LANES = 128
CORES = 2
SCALE = SHARPNESS * math.log2(math.e)
ROOT = math.sqrt(2.0 * SCALE)

F32 = jnp.float32
BF16 = jnp.bfloat16
I32 = jnp.int32


def nt(a, b):
    return lax.dot_general(a, b, (((1,), (1,)), ((), ())), preferred_element_type=F32)


def nn(a, b):
    return lax.dot_general(a, b, (((1,), (0,)), ((), ())), preferred_element_type=F32)


def split2(x):
    hi = x.astype(BF16)
    return hi, (x - hi.astype(F32)).astype(BF16)


def iota(shape, dim):
    return lax.broadcasted_iota(I32, shape, dim)


def fdiv(x, by):
    return jnp.floor((x.astype(F32) + 0.5) * (1.0 / by)).astype(I32)


def prepare(x, y, z, w):
    norm = SCALE * (x * x + y * y + z * z)
    return x * ROOT, y * ROOT, z * ROOT, w * jnp.exp2(-norm)


def self_overlap(ref, lanes, atoms):
    blocks = atoms // 8
    comp = [[ref[pl.ds(c * atoms + 8 * i, 8), lanes] for i in range(blocks)] for c in range(4)]
    total = None
    diag = [None] * blocks
    off = [None] * blocks
    for a in range(atoms):
        xa, ya, za, wa = (ref[pl.ds(c * atoms + a, 1), lanes] for c in range(4))
        wa2 = wa + wa
        for i in range(a // 8, blocks):
            e = jnp.exp2(xa * comp[0][i] + ya * comp[1][i] + za * comp[2][i])
            if i == a // 8:
                diag[i] = wa * e if diag[i] is None else diag[i] + wa * e
            else:
                off[i] = wa2 * e if off[i] is None else off[i] + wa2 * e
    for i in range(blocks):
        part = diag[i] if off[i] is None else diag[i] + off[i]
        part = part * comp[3][i]
        total = part if total is None else total + part
    return jnp.sum(total, axis=0, keepdims=True)


def cross_overlap(qref, cref, lanes, atoms):
    comp = [cref[pl.ds(c * atoms, atoms), lanes] for c in range(4)]
    acc = None
    for a in range(atoms):
        xa, ya, za, wa = (qref[pl.ds(c * atoms + a, 1), lanes] for c in range(4))
        e = wa * jnp.exp2(xa * comp[0] + ya * comp[1] + za * comp[2])
        acc = e if acc is None else acc + e
    return jnp.sum(acc * comp[3], axis=0, keepdims=True)


def kernel(
    nq, nl, cap, id_bytes,
    qp_hbm, lib_hbm, qa_hbm, conf_hbm, cand_hbm, count_hbm, home_hbm,
    tv_hbm, out_ref,
    tv_ref,
    qp_ref, qa_ref, cand_ref, count_ref, home_ref,
    lib, conf, gath, pack, atoms_in, bucket, mid, codes_in, ret_out, mid_back, ret_in,
    confp, qprep, pairs_c, pairs_q, onehot, qonehot, cself, qself, shape_s, valid_s,
    loc_sem, s1_send, s1_recv, sib_send, sib_recv, s2_send, s2_recv,
    send_a, recv_a, send_b, recv_b,
):
    q = lax.axis_index("qry")
    l = lax.axis_index("lib")
    dev = nq * nl
    me = q * nl + l
    nz = nq // CORES
    z, c = q // CORES, lax.rem(q, CORES)
    sib = z * CORES + (1 - c)
    own_rows = lib.shape[0]
    block = qp_ref.shape[0]
    cols = gath.shape[2]
    local_q, listed = cand_ref.shape
    cand_n = local_q * listed
    atoms = qa_ref.shape[1] // 4
    half = 2 * atoms
    pairs = onehot.shape[1]

    def wrap(x, n):
        return jnp.where(x >= n, x - n, x)

    lib_peers = [wrap(l + e, nl) for e in range(1, nl)]
    qry_peers = [wrap(q + d, nq) for d in range(1, nq)]

    def take(ref, sem):
        pltpu.make_async_copy(ref, ref, sem).wait()

    barrier = pltpu.get_barrier_semaphore()

    for tq, tl in [(q, t) for t in lib_peers] + [(t, l) for t in qry_peers]:
        pl.semaphore_signal(
            barrier, inc=1, device_id={"qry": tq, "lib": tl}, device_id_type=pl.DeviceIdType.MESH
        )

    loads = [
        pltpu.make_async_copy(src, dst, loc_sem.at[2 + n])
        for n, (src, dst) in enumerate(
            ((qa_hbm, qa_ref), (cand_hbm, cand_ref), (home_hbm, home_ref), (qp_hbm, qp_ref), (count_hbm, count_ref))
        )
    ]
    for load in loads:
        load.start()
    lib_copy = pltpu.make_async_copy(lib_hbm, lib, loc_sem.at[0])
    conf_copy = pltpu.make_async_copy(conf_hbm, conf, loc_sem.at[1])
    conf_copy.start()
    lib_copy.start()

    for load in loads:
        load.wait()

    qa = qa_ref[...]
    zero = jnp.zeros((local_q, LANES - half), F32)
    top = jnp.concatenate([qa[:, :half], zero], axis=1)
    low = jnp.concatenate([qa[:, half:], zero], axis=1)
    pack[...] = jnp.concatenate([top, low], axis=0).astype(BF16)

    ids = jnp.concatenate([cand_ref[pl.ds(i, 1), :] for i in range(local_q)], axis=1)
    table = home_ref[...]
    trows = table.shape[0]
    pieces = [
        jnp.transpose(((table >> (8 * k)) & 255).astype(F32)).astype(BF16) for k in range(id_bytes)
    ]
    row_hot = jnp.where(iota((trows, cand_n), 0) == (ids >> 7), 1.0, 0.0).astype(BF16)
    lane_hot = iota((LANES, cand_n), 0) == (ids & 127)
    stored = jnp.zeros((1, cand_n), I32)
    for k in range(id_bytes):
        found = nn(pieces[k], row_hot)
        byte = jnp.sum(jnp.where(lane_hot, found, 0.0), axis=0, keepdims=True)
        stored = stored + (byte.astype(I32) << (8 * k))
    owner = fdiv(stored, own_rows)
    slot = stored - owner * own_rows

    pl.semaphore_wait(barrier, nq + nl - 2)

    def remote(src, dst, ssem, rsem, dq, dl):
        return pltpu.make_async_remote_copy(
            src_ref=src, dst_ref=dst, send_sem=ssem, recv_sem=rsem,
            device_id={"qry": dq, "lib": dl}, device_id_type=pl.DeviceIdType.MESH,
        )

    def piece(bq, k):
        return gath.at[k, pl.ds(pl.multiple_of(bq * block, block), block), :]

    def stage1(d):
        return remote(
            qp_ref.at[:, pl.ds(pl.multiple_of(l * cols, cols), cols)], piece(q, l),
            s1_send, s1_recv.at[d], lax.rem(z + d, nz) * CORES + c, l,
        )

    def from_z(d):
        return lax.rem(z - d + nz, nz) * CORES + c

    def stage2(d, e):
        there = piece(from_z(d), l)
        return remote(there, there, s2_send, s2_recv.at[d, e], q, lax.rem(l + e, nl))

    def to_sib(bq, k):
        there = piece(bq, k)
        return remote(there, there, sib_send, sib_recv, sib, l)

    def from_l(e):
        return lax.rem(l - e + nl, nl)

    for d in range(1, nz):
        stage1(d).start()
    for k in range(nl):
        gath[k, pl.ds(pl.multiple_of(q * block, block), block), :] = qp_ref[:, k * cols : (k + 1) * cols]
    for k in range(nl):
        to_sib(q, k).start()

    for t in qry_peers:
        remote(pack, atoms_in.at[q, l], send_a.at[0], recv_a.at[0], t, l).start()
    atoms_in[q, l] = pack[...]

    owns = iota((dev, cand_n), 0) == owner
    owns_b = jnp.where(owns, 1.0, 0.0).astype(BF16)
    tri = jnp.where(iota((cand_n, cand_n), 0) < iota((cand_n, cand_n), 1), 1.0, 0.0).astype(BF16)
    before = nn(owns_b, tri)
    rank = jnp.sum(jnp.where(owns, before, 0.0), axis=0, keepdims=True).astype(I32)
    rank_hot = iota((LANES, cand_n), 0) == rank
    rank_b = jnp.where(rank_hot, 1.0, 0.0).astype(BF16)
    code = slot * local_q + fdiv(iota((1, cand_n), 1), listed) + 1
    lo = (code & 127).astype(F32)
    hi = (code >> 7).astype(F32)
    left = jnp.concatenate([jnp.where(owns, lo, 0.0), jnp.where(owns, hi, 0.0)], axis=0).astype(BF16)
    sums = nt(left, rank_b).astype(I32)
    codes = sums[:dev] + (sums[dev:] << 7)
    for o in range(dev):
        bucket[o // nq, o % nq] = codes[o : o + 1]

    for t in lib_peers:
        remote(bucket.at[t], mid.at[l], send_a.at[1], recv_a.at[1], q, t).start()
    mid[l] = bucket[l]

    conf_copy.wait()
    comps = prepare(*(conf[i * atoms : (i + 1) * atoms] for i in range(4)))
    for i in range(4):
        confp[i * atoms : (i + 1) * atoms] = comps[i]

    q_rest = pl.ds(0, nq - 1)
    l_rest = pl.ds(0, nl - 1)
    take(atoms_in.at[q_rest, 0], recv_a.at[0])
    for t in lib_peers:
        remote(atoms_in.at[:, l], atoms_in.at[:, l], send_b.at[0], recv_b.at[0], q, t).start()
    take(mid.at[l_rest], recv_a.at[1])
    for t in qry_peers:
        remote(mid.at[:, t], codes_in.at[q], send_b.at[1], recv_b.at[1], t, l).start()
    for k in range(nl):
        codes_in[q, k] = mid[k, q]

    def self_step(g, carry):
        lanes = pl.ds(pl.multiple_of(g * LANES, LANES), LANES)
        cself[0:1, lanes] = self_overlap(confp, lanes, atoms)
        return carry

    lax.fori_loop(0, own_rows // LANES, self_step, 0)

    for d in range(1, nz):
        stage1(d).wait_recv()
        for e in range(1, nl):
            stage2(d, e).start()
        to_sib(from_z(d), l).start()

    take(codes_in.at[q_rest], recv_b.at[1])
    take(atoms_in.at[:, l_rest], recv_b.at[0])

    got = codes_in[...].reshape(dev, LANES)
    pair_at = iota((1, pairs), 1)
    pair_src = fdiv(pair_at, cap)
    pair_j = pair_at - pair_src * cap
    j_hot = jnp.where(iota((LANES, pairs), 0) == pair_j, 1.0, 0.0).astype(BF16)
    src_hot = iota((dev, pairs), 0) == pair_src
    both = jnp.concatenate([got & 127, got >> 7], axis=0).astype(F32).astype(BF16)
    spread = nn(both, j_hot)
    low7 = jnp.sum(jnp.where(src_hot, spread[:dev], 0.0), axis=0, keepdims=True).astype(I32)
    high = jnp.sum(jnp.where(src_hot, spread[dev:], 0.0), axis=0, keepdims=True).astype(I32)
    pcode = low7 + (high << 7)
    valid_s[...] = jnp.where(pcode > 0, 1.0, 0.0)
    pcode = jnp.maximum(pcode - 1, 0)
    pslot = fdiv(pcode, local_q)
    pquery = pair_src * local_q + (pcode - pslot * local_q)
    onehot[...] = jnp.where(iota((own_rows, pairs), 0) == pslot, 1.0, 0.0).astype(BF16)
    qonehot[...] = jnp.where(iota((dev * local_q, pairs), 0) == pquery, 1.0, 0.0).astype(BF16)

    raw = atoms_in[...].reshape(dev, 2 * local_q, LANES).astype(F32)
    q_top = jnp.transpose(raw[:, :local_q].reshape(dev * local_q, LANES))
    q_low = jnp.transpose(raw[:, local_q:].reshape(dev * local_q, LANES))
    comps = prepare(q_top[:atoms], q_top[atoms:half], q_low[:atoms], q_low[atoms:half])
    for i in range(4):
        qprep[i * atoms : (i + 1) * atoms] = comps[i]

    def qself_step(g, carry):
        lanes = pl.ds(pl.multiple_of(g * LANES, LANES), LANES)
        qself[0:1, lanes] = self_overlap(qprep, lanes, atoms)
        return carry

    lax.fori_loop(0, dev * local_q // LANES, qself_step, 0)

    pad = jnp.zeros((7, own_rows), F32)
    hi_c, lo_c = split2(jnp.concatenate([confp[...], cself[...], pad], axis=0))
    pairs_c[...] = nn(hi_c, onehot[...]) + nn(lo_c, onehot[...])
    pad = jnp.zeros((7, dev * local_q), F32)
    hi_q, lo_q = split2(jnp.concatenate([qprep[...], qself[...], pad], axis=0))
    pairs_q[...] = nn(hi_q, qonehot[...]) + nn(lo_q, qonehot[...])

    def cross_step(g, carry):
        lanes = pl.ds(pl.multiple_of(g * LANES, LANES), LANES)
        cross = cross_overlap(pairs_q, pairs_c, lanes, atoms)
        selves = pairs_q[4 * atoms : 4 * atoms + 1, lanes] + pairs_c[4 * atoms : 4 * atoms + 1, lanes]
        shape_s[0:1, lanes] = cross / (selves - cross)
        return carry

    groups = pairs // LANES
    first = groups // 3
    lax.fori_loop(0, first, cross_step, 0)

    for d in range(1, nz):
        for e in range(1, nl):
            stage2(d, e).wait_recv()
            to_sib(from_z(d), from_l(e)).start()

    lax.fori_loop(first, groups, cross_step, 0)

    take(gath.at[:, pl.ds(0, nz * block), :], sib_recv)
    lib_copy.wait()

    rows = nq * block
    chunk = min(rows, 256)
    priors = None
    for r in range(0, rows, chunk):
        scores = None
        norms = None
        for k in range(nl):
            part = gath[k, r : r + chunk, :]
            prod = nt(part, lib[:, k * cols : (k + 1) * cols])
            wide = part.astype(F32)
            sq = jnp.sum(wide * wide, axis=1, keepdims=True)
            scores = prod if scores is None else scores + prod
            norms = sq if norms is None else norms + sq
        tv = (scores * (1.0 / (norms + EPSILON))).astype(BF16)
        tv_ref[r : r + chunk, :] = tv
        chosen = nn(tv, onehot[...]) * qonehot[r : r + chunk, :].astype(F32)
        chosen = jnp.sum(chosen, axis=0, keepdims=True)
        priors = chosen if priors is None else priors + chosen

    tv_copy = pltpu.make_async_copy(tv_ref, tv_hbm, loc_sem.at[7])
    tv_copy.start()
    score = jnp.where(valid_s[...] > 0.0, shape_s[...] + priors, 0.0)
    hi_s, lo_s = split2(jnp.where(src_hot, score, 0.0))
    back = nt(hi_s, j_hot) + nt(lo_s, j_hot)
    for s in range(dev):
        ret_out[s // nl, s % nl] = back[s : s + 1]

    for t in qry_peers:
        remote(ret_out.at[t], mid_back.at[q], send_a.at[2], recv_a.at[2], t, l).start()
    mid_back[q] = ret_out[q]
    take(mid_back.at[q_rest], recv_a.at[2])
    for t in lib_peers:
        remote(mid_back.at[:, t], ret_in.at[l], send_b.at[2], recv_b.at[2], q, t).start()
    for k in range(nq):
        ret_in[l, k] = mid_back[k, l]

    take(gath.at[0, pl.ds(0, (nz - 1) * block), :], s1_send)
    take(gath.at[pl.ds(0, nl - 1), pl.ds(0, (nz - 1) * block), :], s2_send)
    take(gath.at[:, pl.ds(0, nz * block), :], sib_send)
    take(atoms_in.at[q_rest, 0], send_a.at[0])
    take(mid.at[l_rest], send_a.at[1])
    take(mid_back.at[q_rest], send_a.at[2])
    take(atoms_in.at[:, l_rest], send_b.at[0])
    take(codes_in.at[q_rest], send_b.at[1])
    take(ret_in.at[l_rest], recv_b.at[2])

    came = jnp.transpose(ret_in[...].reshape(dev, LANES))
    hi_b, lo_b = split2(came)
    mine = nn(hi_b, owns_b) + nn(lo_b, owns_b)
    final = jnp.sum(jnp.where(rank_hot, mine, 0.0), axis=0, keepdims=True)
    for i in range(local_q):
        line = final[:, i * listed : (i + 1) * listed]
        live = iota((1, listed), 1) < count_ref[i]
        out_ref[i : i + 1, :] = jnp.where(live, line, 0.0)

    take(ret_in.at[l_rest], send_b.at[2])
    tv_copy.wait()


def body(nq, nl, query_prints, library_prints, query_atoms, conformer_atoms, candidates, candidate_count, home_row):
    dev = nq * nl
    block, width = query_prints.shape
    own_rows = library_prints.shape[0]
    local_q, listed = candidates.shape
    atoms = query_atoms.shape[1] // 4
    cand_n = local_q * listed
    cap = 2 * ((cand_n + dev - 1) // dev) + 4
    pairs = (dev * cap + LANES - 1) // LANES * LANES
    id_bytes = ((home_row.shape[0] - 1).bit_length() + 7) // 8
    rows = nq * block
    nz = nq // CORES
    limit = 56 * 1024 * 1024
    vm = pltpu.VMEM
    dma = pltpu.SemaphoreType.DMA
    vspec = pl.BlockSpec(memory_space=pltpu.VMEM)
    return pl.pallas_call(
        functools.partial(kernel, nq, nl, cap, id_bytes),
        out_shape=(
            jax.ShapeDtypeStruct((rows, own_rows), BF16),
            jax.ShapeDtypeStruct((local_q, listed), F32),
        ),
        in_specs=[pl.BlockSpec(memory_space=pltpu.HBM)] * 7,
        out_specs=(pl.BlockSpec(memory_space=pl.ANY), vspec),
        scratch_shapes=[
            vm((rows, own_rows), BF16),
            vm((block, width), BF16),
            vm((local_q, 4 * atoms), F32),
            vm((local_q, listed), I32),
            pltpu.SMEM((local_q,), I32),
            vm((home_row.shape[0] // LANES, LANES), I32),
            vm((own_rows, width), BF16),
            vm((4 * atoms, own_rows), F32),
            vm((nl, rows, width // nl), BF16),
            vm((2 * local_q, LANES), BF16),
            vm((nq, nl, 2 * local_q, LANES), BF16),
            vm((nl, nq, 1, LANES), I32),
            vm((nl, nq, 1, LANES), I32),
            vm((nq, nl, 1, LANES), I32),
            vm((nq, nl, 1, LANES), F32),
            vm((nq, nl, 1, LANES), F32),
            vm((nl, nq, 1, LANES), F32),
            vm((4 * atoms, own_rows), F32),
            vm((4 * atoms, rows), F32),
            vm((4 * atoms + 8, pairs), F32),
            vm((4 * atoms + 8, pairs), F32),
            vm((own_rows, pairs), BF16),
            vm((rows, pairs), BF16),
            vm((1, own_rows), F32),
            vm((1, rows), F32),
            vm((1, pairs), F32),
            vm((1, pairs), F32),
            dma((8,)),
            dma, dma((nz,)),
            dma, dma,
            dma, dma((nz, nl)),
            dma((3,)), dma((3,)),
            dma((3,)), dma((3,)),
        ],
        compiler_params=pltpu.CompilerParams(
            collective_id=0, has_side_effects=True, vmem_limit_bytes=limit
        ),
    )(
        query_prints, library_prints, query_atoms, conformer_atoms.T, candidates, candidate_count,
        home_row.reshape(-1, LANES),
    )


def solution(mesh):
    return jax.shard_map(
        functools.partial(body, mesh.shape["qry"], mesh.shape["lib"]),
        mesh=mesh,
        in_specs=(
            P("qry", None),
            P(("lib", "qry"), None),
            P(("qry", "lib"), None),
            P(("lib", "qry"), None),
            P(("qry", "lib"), None),
            P(("qry", "lib")),
            P(),
        ),
        out_specs=(P(None, ("lib", "qry")), P(("qry", "lib"), None)),
        check_vma=False,
    )
```

profile of v0, /device:TPU:0, one launch (start us, length us, event | category | flops | bytes accessed | tf_op | source)
XLA Modules:
  0.0 34.8 jit_solution(13599801158474610621)
XLA Ops:
  0.6 31.1 %shard_map.86 = (bf16[256,768]{1,0:T(8,128)(2,1)}, f32[8,64]{1,0:T(8,128)}) custom-call(bf16[32,2048]{1,0:T(8,128)(2,1)} %qp_hbm.1, bf16[768,2048]{1,0:T(8,128)(2,1)} %lib_hbm.1, f32[8,192]{1,0:T(8,128)} %qa_hbm.1, f32[192,768]{1,0:T(8,128)} %bitcast.2, s32[8,64]{1,0:T(8,128)} %cand_hbm.1, s32[8]{0:T(128)} %count_hbm.1, s32[192,128]{1,0:T(8,128)} %bitcast.3), custom_call_target="tpu_custom_call" | custom-call | tf_op jit(solution)/shard_map/pallas_call | solution.py:391
  31.8 1.8 %copy.11 = bf16[256,768]{1,0:T(8,128)(2,1)} copy(bf16[256,768]{1,0:T(8,128)(2,1)} %get-tuple-element.4) | data formatting | bytes 786432
  33.6 1.3 %copy.12 = f32[8,64]{1,0:T(8,128)} copy(f32[8,64]{1,0:T(8,128)} %get-tuple-element.5) | data formatting | bytes 4096
where the time goes:
time: 35.1 us; the launch traced here: 34.8 us
  Pallas kernels  31.1 us (89%)
  local copies, waits for them, and re-layouts  3.03 us (9%)
  between operations  0.64 us (2%)
    pallas_call x1, Pallas kernels, body(): pl.pallas_call(functools.partial(kernel, nq, nl, cap, id_bytes), out_shap...  31.1 us
    unnamed x2, local copies, waits for them, and re-layouts  3.03 us

commit v1 on v0

v1 whole, which is shorter than its diff:
```python
import functools
import math

import jax
import jax.numpy as jnp
from jax import lax
from jax.experimental import pallas as pl
from jax.experimental.pallas import tpu as pltpu
from jax.sharding import PartitionSpec as P

SHARPNESS = 0.8
EPSILON = 1e-06
LANES = 128
CORES = 2
SCALE = SHARPNESS * math.log2(math.e)
ROOT = math.sqrt(2.0 * SCALE)

F32 = jnp.float32
BF16 = jnp.bfloat16
I32 = jnp.int32


def nt(a, b):
    return lax.dot_general(a, b, (((1,), (1,)), ((), ())), preferred_element_type=F32)


def nn(a, b):
    return lax.dot_general(a, b, (((1,), (0,)), ((), ())), preferred_element_type=F32)


def split2(x):
    hi = x.astype(BF16)
    return hi, (x - hi.astype(F32)).astype(BF16)


def iota(shape, dim):
    return lax.broadcasted_iota(I32, shape, dim)


def fdiv(x, by):
    return jnp.floor((x.astype(F32) + 0.5) * (1.0 / by)).astype(I32)


def prepare(x, y, z, w):
    norm = SCALE * (x * x + y * y + z * z)
    return x * ROOT, y * ROOT, z * ROOT, w * jnp.exp2(-norm)


def self_overlap(ref, lanes, atoms):
    blocks = atoms // 8
    comp = [[ref[pl.ds(c * atoms + 8 * i, 8), lanes] for i in range(blocks)] for c in range(4)]
    total = None
    diag = [None] * blocks
    off = [None] * blocks
    for a in range(atoms):
        xa, ya, za, wa = (ref[pl.ds(c * atoms + a, 1), lanes] for c in range(4))
        wa2 = wa + wa
        for i in range(a // 8, blocks):
            e = jnp.exp2(xa * comp[0][i] + ya * comp[1][i] + za * comp[2][i])
            if i == a // 8:
                diag[i] = wa * e if diag[i] is None else diag[i] + wa * e
            else:
                off[i] = wa2 * e if off[i] is None else off[i] + wa2 * e
    for i in range(blocks):
        part = diag[i] if off[i] is None else diag[i] + off[i]
        part = part * comp[3][i]
        total = part if total is None else total + part
    return jnp.sum(total, axis=0, keepdims=True)


def cross_overlap(qref, cref, lanes, atoms):
    comp = [cref[pl.ds(c * atoms, atoms), lanes] for c in range(4)]
    acc = None
    for a in range(atoms):
        xa, ya, za, wa = (qref[pl.ds(c * atoms + a, 1), lanes] for c in range(4))
        e = wa * jnp.exp2(xa * comp[0] + ya * comp[1] + za * comp[2])
        acc = e if acc is None else acc + e
    return jnp.sum(acc * comp[3], axis=0, keepdims=True)


def flip(x, bits):
    step, out = 1, x
    while step < 256:
        one = lax.rem(lax.div(x, step), 2)
        other = lax.rem(lax.div(bits, step), 2) if not isinstance(bits, int) else (bits // step) % 2
        out = out + other * (1 - 2 * one) * step
        step *= 2
        if isinstance(bits, int) and step > bits:
            break
    return out


def kernel(
    nq, nl, cap, id_bytes,
    qp_hbm, lib_hbm, qa_hbm, conf_hbm, cand_hbm, count_hbm, home_hbm,
    tv_hbm, out_ref,
    tv_ref,
    qp_ref, qa_ref, cand_ref, count_ref, home_ref,
    lib, conf, gath, pack, atoms_in, codes_out, codes_in, score, ret_in,
    confp, qprep, ownprep, pairs_c, pairs_q, onehot, qonehot, cself, shape_s,
    loc_sem, s1_send, s1_recv, sib_send, sib_recv, s2_send, s2_recv,
    send_a, recv_a, send_b, recv_b, send_c, recv_c, send_d, recv_d,
):
    q = lax.axis_index("qry")
    l = lax.axis_index("lib")
    dev = nq * nl
    me = q * nl + l
    me_o = l * nq + q
    nz = nq // CORES
    z, c = lax.div(q, CORES), lax.rem(q, CORES)
    sib = z * CORES + (1 - c)
    own_rows = lib.shape[0]
    block = qp_ref.shape[0]
    cols = gath.shape[2]
    local_q, listed = cand_ref.shape
    cand_n = local_q * listed
    atoms = qa_ref.shape[1] // 4
    half = 2 * atoms
    pairs = onehot.shape[1]
    groups = pairs // LANES

    spread = [(d, e) for d in range(nq) for e in range(nl) if d or e]
    spread.sort(key=lambda o: -(o[0] // CORES + bin(o[1]).count("1")))
    peers = [(flip(q, d) if d else q, flip(l, e) if e else l) for d, e in spread]
    lib_peers = [flip(l, e) for e in range(1, nl)]
    qry_peers = [flip(q, d) for d in range(nq - 1, 0, -1)]

    def take(ref, sem):
        pltpu.make_async_copy(ref, ref, sem).wait()

    def remote(src, dst, ssem, rsem, dq, dl):
        return pltpu.make_async_remote_copy(
            src_ref=src, dst_ref=dst, send_sem=ssem, recv_sem=rsem,
            device_id={"qry": dq, "lib": dl}, device_id_type=pl.DeviceIdType.MESH,
        )

    barrier = pltpu.get_barrier_semaphore()
    loads = [
        pltpu.make_async_copy(src, dst, loc_sem.at[2 + n])
        for n, (src, dst) in enumerate(
            ((qa_hbm, qa_ref), (cand_hbm, cand_ref), (home_hbm, home_ref), (qp_hbm, qp_ref), (count_hbm, count_ref))
        )
    ]
    for load in loads:
        load.start()
    lib_copy = pltpu.make_async_copy(lib_hbm, lib, loc_sem.at[0])
    conf_copy = pltpu.make_async_copy(conf_hbm, conf, loc_sem.at[1])
    conf_copy.start()
    lib_copy.start()

    for tq, tl in peers:
        pl.semaphore_signal(
            barrier, inc=1, device_id={"qry": tq, "lib": tl}, device_id_type=pl.DeviceIdType.MESH
        )

    for load in loads:
        load.wait()

    ids = jnp.concatenate([cand_ref[pl.ds(i, 1), :] for i in range(local_q)], axis=1)
    table = home_ref[...]
    trows = table.shape[0]
    pieces = [
        jnp.transpose(((table >> (8 * k)) & 255).astype(F32)).astype(BF16) for k in range(id_bytes)
    ]
    row_hot = jnp.where(iota((trows, cand_n), 0) == (ids >> 7), 1.0, 0.0).astype(BF16)
    lane_hot = iota((LANES, cand_n), 0) == (ids & 127)
    stored = jnp.zeros((1, cand_n), I32)
    for k in range(id_bytes):
        found = nn(pieces[k], row_hot)
        byte = jnp.sum(jnp.where(lane_hot, found, 0.0), axis=0, keepdims=True)
        stored = stored + (byte.astype(I32) << (8 * k))
    owner = fdiv(stored, own_rows)
    slot = stored - owner * own_rows

    owns = iota((dev, cand_n), 0) == owner
    owns_b = jnp.where(owns, 1.0, 0.0).astype(BF16)
    tri = jnp.where(iota((cand_n, cand_n), 0) < iota((cand_n, cand_n), 1), 1.0, 0.0).astype(BF16)
    before = nn(owns_b, tri)
    rank = jnp.sum(jnp.where(owns, before, 0.0), axis=0, keepdims=True).astype(I32)
    my_off = lax.rem(cap * me, LANES)
    rank_b = jnp.where(iota((2 * LANES, cand_n), 0) == rank + my_off, 1.0, 0.0).astype(BF16)
    code = slot * local_q + fdiv(iota((1, cand_n), 1), listed) + 1
    lo = (code & 127).astype(F32)
    hi = (code >> 7).astype(F32)
    left = jnp.concatenate([jnp.where(owns, lo, 0.0), jnp.where(owns, hi, 0.0)], axis=0).astype(BF16)
    sums = nt(left, rank_b).astype(I32)
    codes = sums[:dev] + (sums[dev:] << 7)
    for o in range(dev):
        for k in range(2):
            codes_out[o, k] = codes[o : o + 1, k * LANES : (k + 1) * LANES]

    qa = qa_ref[...]
    zero = jnp.zeros((local_q, LANES - half), F32)
    top = jnp.concatenate([qa[:, :half], zero], axis=1)
    low = jnp.concatenate([qa[:, half:], zero], axis=1)
    fill = jnp.zeros((LANES - local_q, LANES), F32)
    top_t = jnp.transpose(jnp.concatenate([top, fill], axis=0))
    low_t = jnp.transpose(jnp.concatenate([low, fill], axis=0))
    comps = prepare(top_t[:atoms], top_t[atoms:half], low_t[:atoms], low_t[atoms:half])
    for i in range(4):
        ownprep[i * atoms : (i + 1) * atoms] = comps[i]
    own_self = self_overlap(ownprep, pl.ds(0, LANES), atoms)
    lane_at = iota((local_q, LANES), 1)
    own_col = jnp.sum(
        jnp.where(lane_at == iota((local_q, LANES), 0), own_self, 0.0), axis=1, keepdims=True
    )
    own_hi = own_col.astype(BF16).astype(F32)
    low = jnp.where(lane_at == half, own_hi, jnp.where(lane_at == half + 1, own_col - own_hi, low))
    pack[...] = jnp.concatenate([top, low], axis=0).astype(BF16)

    pl.semaphore_wait(barrier, dev - 1)

    def piece(bq, k):
        return gath.at[k, pl.ds(pl.multiple_of(bq * block, block), block), :]

    def from_z(d):
        return flip(z, d) * CORES + c

    def stage1(d):
        return remote(
            qp_ref.at[:, pl.ds(pl.multiple_of(l * cols, cols), cols)], piece(q, l),
            s1_send, s1_recv.at[d], from_z(d), l,
        )

    def stage2(d, e):
        there = piece(from_z(d), l)
        return remote(there, there, s2_send, s2_recv.at[d, e], q, flip(l, e))

    def to_sib(bq, k):
        there = piece(bq, k)
        return remote(there, there, sib_send, sib_recv, sib, l)

    for d in range(1, nz):
        stage1(d).start()
    for t in qry_peers:
        remote(pack, atoms_in.at[q, l], send_a, recv_a, t, l).start()
    for tq, tl in peers:
        remote(codes_out.at[tl * nq + tq], codes_in.at[me], send_c, recv_c, tq, tl).start()
    for k in range(nl):
        gath[k, pl.ds(pl.multiple_of(q * block, block), block), :] = qp_ref[:, k * cols : (k + 1) * cols]
    for k in range(nl):
        to_sib(q, k).start()
    atoms_in[q, l] = pack[...]
    codes_in[me] = codes_out[me_o]

    conf_copy.wait()
    comps = prepare(*(conf[i * atoms : (i + 1) * atoms] for i in range(4)))
    for i in range(4):
        confp[i * atoms : (i + 1) * atoms] = comps[i]

    def self_step(g, carry):
        lanes = pl.ds(pl.multiple_of(g * LANES, LANES), LANES)
        cself[0:1, lanes] = self_overlap(confp, lanes, atoms)
        return carry

    lax.fori_loop(0, own_rows // LANES, self_step, 0)

    q_rest = pl.ds(0, nq - 1)
    l_rest = pl.ds(0, nl - 1)
    d_rest = pl.ds(0, dev - 1)

    for d in range(1, nz):
        stage1(d).wait_recv()
        for e in range(nl - 1, 0, -1):
            stage2(d, e).start()
        to_sib(from_z(d), l).start()
        if d == 1:
            take(atoms_in.at[q_rest, 0], recv_a)
            for t in lib_peers:
                remote(atoms_in.at[:, l], atoms_in.at[:, l], send_b, recv_b, q, t).start()

    take(codes_in.at[d_rest], recv_c)
    parts = [None] * groups
    for s in range(dev):
        g = cap * s // LANES
        for k in range(2):
            if g + k < groups:
                row = codes_in[s, k]
                parts[g + k] = row if parts[g + k] is None else parts[g + k] + row
    none = jnp.zeros((1, LANES), I32)
    pcode = jnp.concatenate([none if p is None else p for p in parts], axis=1)
    valid = pcode > 0
    pcode = jnp.maximum(pcode - 1, 0)
    pslot = fdiv(pcode, local_q)
    pquery = fdiv(iota((1, pairs), 1), cap) * local_q + (pcode - pslot * local_q)
    onehot[...] = jnp.where(iota((own_rows, pairs), 0) == pslot, 1.0, 0.0).astype(BF16)
    qonehot[...] = jnp.where(iota((dev * local_q, pairs), 0) == pquery, 1.0, 0.0).astype(BF16)

    pad = jnp.zeros((7, own_rows), F32)
    hi_c, lo_c = split2(jnp.concatenate([confp[...], cself[...], pad], axis=0))
    pairs_c[...] = nn(hi_c, onehot[...]) + nn(lo_c, onehot[...])

    take(atoms_in.at[:, l_rest], recv_b)
    raw = atoms_in[...].reshape(dev, 2 * local_q, LANES).astype(F32)
    q_top = jnp.transpose(raw[:, :local_q].reshape(dev * local_q, LANES))
    q_low = jnp.transpose(raw[:, local_q:].reshape(dev * local_q, LANES))
    comps = prepare(q_top[:atoms], q_top[atoms:half], q_low[:atoms], q_low[atoms:half])
    for i in range(4):
        qprep[i * atoms : (i + 1) * atoms] = comps[i]
    qself = q_low[half : half + 1] + q_low[half + 1 : half + 2]
    pad = jnp.zeros((7, dev * local_q), F32)
    hi_q, lo_q = split2(jnp.concatenate([qprep[...], qself, pad], axis=0))
    pairs_q[...] = nn(hi_q, qonehot[...]) + nn(lo_q, qonehot[...])

    n_far = (nz - 1) * (nl - 1)
    each = (n_far + groups - 1) // groups

    def onward(n):
        d = 1 + lax.div(n, nl - 1)
        e = nl - 1 - lax.rem(n, nl - 1)
        stage2(d, e).wait_recv()
        to_sib(from_z(d), flip(l, e)).start()

    def cross_step(g, carry):
        for k in range(each):
            n = g * each + k
            if groups * each == n_far:
                onward(n)
            else:
                pl.when(n < n_far)(functools.partial(onward, n))
        lanes = pl.ds(pl.multiple_of(g * LANES, LANES), LANES)
        cross = cross_overlap(pairs_q, pairs_c, lanes, atoms)
        selves = pairs_q[4 * atoms : 4 * atoms + 1, lanes] + pairs_c[4 * atoms : 4 * atoms + 1, lanes]
        shape_s[0:1, lanes] = cross / (selves - cross)
        return carry

    lax.fori_loop(0, groups, cross_step, 0)

    take(gath.at[:, pl.ds(0, nz * block), :], sib_recv)
    lib_copy.wait()

    rows = nq * block
    chunk = min(rows, 256)
    for r in range(0, rows, chunk):
        scores = None
        norms = None
        for k in range(nl):
            part = gath[k, r : r + chunk, :]
            prod = nt(part, lib[:, k * cols : (k + 1) * cols])
            wide = part.astype(F32)
            sq = jnp.sum(wide * wide, axis=1, keepdims=True)
            scores = prod if scores is None else scores + prod
            norms = sq if norms is None else norms + sq
        tv_ref[r : r + chunk, :] = (scores * (1.0 / (norms + EPSILON))).astype(BF16)

    tv_copy = pltpu.make_async_copy(tv_ref, tv_hbm, loc_sem.at[7])
    tv_copy.start()
    for g in range(groups):
        first = LANES * g // cap * local_q // 16 * 16
        last = min((LANES * g + LANES - 1) // cap * local_q // 16 * 16 + 16, rows)
        lanes = slice(g * LANES, (g + 1) * LANES)
        chosen = nn(tv_ref[first:last, :], onehot[:, lanes])
        mine = iota((last - first, LANES), 0) + first == pquery[:, lanes]
        prior = jnp.sum(jnp.where(mine, chosen, 0.0), axis=0, keepdims=True)
        score[g] = jnp.where(valid[:, lanes], shape_s[:, lanes] + prior, 0.0)
    score[groups] = jnp.zeros((1, LANES), F32)

    for tq, tl in peers:
        at = lax.div(cap * (tq * nl + tl), LANES)
        remote(score.at[pl.ds(at, 2)], ret_in.at[me_o], send_d, recv_d, tq, tl).start()
    ret_in[me_o] = score[pl.ds(lax.div(cap * me, LANES), 2)]

    take(gath.at[0, pl.ds(0, (nz - 1) * block), :], s1_send)
    take(gath.at[pl.ds(0, nl - 1), pl.ds(0, (nz - 1) * block), :], s2_send)
    take(gath.at[:, pl.ds(0, nz * block), :], sib_send)
    take(atoms_in.at[q_rest, 0], send_a)
    take(atoms_in.at[:, l_rest], send_b)
    take(codes_in.at[d_rest], send_c)
    tv_copy.wait()
    take(ret_in.at[d_rest], recv_d)

    came = jnp.concatenate([ret_in[:, k].reshape(dev, LANES) for k in range(2)], axis=1)
    hi_b, lo_b = split2(came)
    mine = nn(hi_b, rank_b) + nn(lo_b, rank_b)
    final = jnp.sum(jnp.where(owns, mine, 0.0), axis=0, keepdims=True)
    for i in range(local_q):
        line = final[:, i * listed : (i + 1) * listed]
        live = iota((1, listed), 1) < count_ref[i]
        out_ref[i : i + 1, :] = jnp.where(live, line, 0.0)

    take(ret_in.at[d_rest], send_d)


def copy_out(tv_in, score_in, tv_out, score_out, sems):
    copies = [
        pltpu.make_async_copy(tv_in, tv_out, sems.at[0]),
        pltpu.make_async_copy(score_in, score_out, sems.at[1]),
    ]
    for copy in copies:
        copy.start()
    for copy in copies:
        copy.wait()


def hand_over(tv, score):
    return pl.pallas_call(
        copy_out,
        out_shape=(jax.ShapeDtypeStruct(tv.shape, tv.dtype), jax.ShapeDtypeStruct(score.shape, score.dtype)),
        in_specs=[pl.BlockSpec(memory_space=pltpu.VMEM)] * 2,
        out_specs=(pl.BlockSpec(memory_space=pl.ANY), pl.BlockSpec(memory_space=pl.ANY)),
        scratch_shapes=[pltpu.SemaphoreType.DMA((2,))],
    )(tv, score)


def body(nq, nl, query_prints, library_prints, query_atoms, conformer_atoms, candidates, candidate_count, home_row):
    dev = nq * nl
    block, width = query_prints.shape
    own_rows = library_prints.shape[0]
    local_q, listed = candidates.shape
    atoms = query_atoms.shape[1] // 4
    cand_n = local_q * listed
    cap = 2 * ((cand_n + dev - 1) // dev) + 4
    pairs = (dev * cap + LANES - 1) // LANES * LANES
    id_bytes = ((home_row.shape[0] - 1).bit_length() + 7) // 8
    rows = nq * block
    nz = nq // CORES
    limit = 56 * 1024 * 1024
    vm = pltpu.VMEM
    dma = pltpu.SemaphoreType.DMA
    vspec = pl.BlockSpec(memory_space=pltpu.VMEM)
    tv, score = pl.pallas_call(
        functools.partial(kernel, nq, nl, cap, id_bytes),
        out_shape=(
            jax.ShapeDtypeStruct((rows, own_rows), BF16),
            jax.ShapeDtypeStruct((local_q, listed), F32),
        ),
        in_specs=[pl.BlockSpec(memory_space=pltpu.HBM)] * 7,
        out_specs=(pl.BlockSpec(memory_space=pl.ANY), vspec),
        scratch_shapes=[
            vm((rows, own_rows), BF16),
            vm((block, width), BF16),
            vm((local_q, 4 * atoms), F32),
            vm((local_q, listed), I32),
            pltpu.SMEM((local_q,), I32),
            vm((home_row.shape[0] // LANES, LANES), I32),
            vm((own_rows, width), BF16),
            vm((4 * atoms, own_rows), F32),
            vm((nl, rows, width // nl), BF16),
            vm((2 * local_q, LANES), BF16),
            vm((nq, nl, 2 * local_q, LANES), BF16),
            vm((dev, 2, 1, LANES), I32),
            vm((dev, 2, 1, LANES), I32),
            vm((pairs // LANES + 1, 1, LANES), F32),
            vm((dev, 2, 1, LANES), F32),
            vm((4 * atoms, own_rows), F32),
            vm((4 * atoms, rows), F32),
            vm((4 * atoms, LANES), F32),
            vm((4 * atoms + 8, pairs), F32),
            vm((4 * atoms + 8, pairs), F32),
            vm((own_rows, pairs), BF16),
            vm((rows, pairs), BF16),
            vm((1, own_rows), F32),
            vm((1, pairs), F32),
            dma((8,)),
            dma, dma((nz,)),
            dma, dma,
            dma, dma((nz, nl)),
            dma, dma, dma, dma, dma, dma, dma, dma,
        ],
        compiler_params=pltpu.CompilerParams(
            collective_id=0, has_side_effects=True, vmem_limit_bytes=limit
        ),
    )(
        query_prints, library_prints, query_atoms, conformer_atoms.T, candidates, candidate_count,
        home_row.reshape(-1, LANES),
    )
    return hand_over(tv, score)


def solution(mesh):
    return jax.shard_map(
        functools.partial(body, mesh.shape["qry"], mesh.shape["lib"]),
        mesh=mesh,
        in_specs=(
            P("qry", None),
            P(("lib", "qry"), None),
            P(("qry", "lib"), None),
            P(("lib", "qry"), None),
            P(("qry", "lib"), None),
            P(("qry", "lib")),
            P(),
        ),
        out_specs=(P(None, ("lib", "qry")), P(("qry", "lib"), None)),
        check_vma=False,
    )
```

time: 35.1 us -> 31.9 us (0.909)
  local copies, waits for them, and re-layouts: 3.03 us -> 0 us
    unnamed x2 -> x0, local copies, waits for them, and re-layouts: 3.03 us -> none
    pallas_call x1, Pallas kernels: 31.1 us -> 29.3 us  [body(): pl.pallas_call(functools.partial(kernel, nq, nl, cap, id_bytes), out_shap...]
    pallas_call x0 -> x1, Pallas kernels: none -> 1.76 us  [hand_over(): pl.pallas_call(copy_out, out_shape=(jax.ShapeDtypeStruct(tv.shape, tv.dty...]
where the time goes in v1:
time: 31.9 us; the launch traced here: 31.7 us
  Pallas kernels  31.1 us (97%)
  between operations  0.64 us (2%)
    pallas_call x1, Pallas kernels, body(): pl.pallas_call(functools.partial(kernel, nq, nl, cap, id_bytes), out_shap...  29.3 us
    pallas_call x1, Pallas kernels, hand_over(): pl.pallas_call(copy_out, out_shape=(jax.ShapeDtypeStruct(tv.shape, tv.dty...  1.76 us

profile of v1, /device:TPU:0, one launch (start us, length us, event | category | flops | bytes accessed | tf_op | source)
XLA Modules:
  0.0 31.7 jit_solution(9641359255357313721)
XLA Ops:
  0.6 29.3 %shard_map.86 = (bf16[256,768]{1,0:T(8,128)(2,1)}, f32[8,64]{1,0:T(8,128)}) custom-call(bf16[32,2048]{1,0:T(8,128)(2,1)} %qp_hbm.1, bf16[768,2048]{1,0:T(8,128)(2,1)} %lib_hbm.1, f32[8,192]{1,0:T(8,128)} %qa_hbm.1, f32[192,768]{1,0:T(8,128)} %bitcast.2, s32[8,64]{1,0:T(8,128)} %cand_hbm.1, s32[8]{0:T(128)} %count_hbm.1, s32[192,128]{1,0:T(8,128)} %bitcast.3), custom_call_target="tpu_custom_call" | custom-call | tf_op jit(solution)/shard_map/pallas_call | solution.py:421
  29.9 1.8 %shard_map.87 = (bf16[256,768]{1,0:T(8,128)(2,1)}, f32[8,64]{1,0:T(8,128)}) custom-call(bf16[256,768]{1,0:T(8,128)(2,1)} %get-tuple-element.4.tv_in, f32[8,64]{1,0:T(8,128)} %get-tuple-element.5.score_in), custom_call_target="tpu_custom_call" | custom-call | tf_op jit(solution)/shard_map/pallas_call | solution.py:396

commit v2 on v1

--- a/solution.py
+++ b/solution.py
@@ -99,7 +99,7 @@
     lib, conf, gath, pack, atoms_in, codes_out, codes_in, score, ret_in,
     confp, qprep, ownprep, pairs_c, pairs_q, onehot, qonehot, cself, shape_s,
     loc_sem, s1_send, s1_recv, sib_send, sib_recv, s2_send, s2_recv,
-    send_a, recv_a, send_b, recv_b, send_c, recv_c, send_d, recv_d,
+    send_a, recv_a, send_b, recv_b, send_c, recv_c, send_d, recv_d, send_e, recv_e, ready,
 ):
     q = lax.axis_index("qry")
     l = lax.axis_index("lib")
@@ -121,9 +121,8 @@
 
     spread = [(d, e) for d in range(nq) for e in range(nl) if d or e]
     spread.sort(key=lambda o: -(o[0] // CORES + bin(o[1]).count("1")))
+    near = [(q, flip(l, e)) for e in range(nl - 1, 0, -1)] + [(flip(q, d), l) for d in range(nq - 1, 0, -1)]
     peers = [(flip(q, d) if d else q, flip(l, e) if e else l) for d, e in spread]
-    lib_peers = [flip(l, e) for e in range(1, nl)]
-    qry_peers = [flip(q, d) for d in range(nq - 1, 0, -1)]
 
     def take(ref, sem):
         pltpu.make_async_copy(ref, ref, sem).wait()
@@ -148,7 +147,7 @@
     conf_copy.start()
     lib_copy.start()
 
-    for tq, tl in peers:
+    for tq, tl in near:
         pl.semaphore_signal(
             barrier, inc=1, device_id={"qry": tq, "lib": tl}, device_id_type=pl.DeviceIdType.MESH
         )
@@ -208,7 +207,11 @@
     low = jnp.where(lane_at == half, own_hi, jnp.where(lane_at == half + 1, own_col - own_hi, low))
     pack[...] = jnp.concatenate([top, low], axis=0).astype(BF16)
 
-    pl.semaphore_wait(barrier, dev - 1)
+    pl.semaphore_wait(barrier, nq + nl - 2)
+    for e in range(nl - 1, 0, -1):
+        pl.semaphore_signal(
+            ready, inc=1, device_id={"qry": q, "lib": flip(l, e)}, device_id_type=pl.DeviceIdType.MESH
+        )
 
     def piece(bq, k):
         return gath.at[k, pl.ds(pl.multiple_of(bq * block, block), block), :]
@@ -230,18 +233,19 @@
         there = piece(bq, k)
         return remote(there, there, sib_send, sib_recv, sib, l)
 
+    def atoms_to(k, dq, dl, ssem, rsem):
+        there = atoms_in.at[k, c]
+        return remote(there, there, ssem, rsem, dq, dl)
+
+    for d in range(nz - 1, 0, -1):
+        remote(pack, atoms_in.at[l, c, z], send_a, recv_a, from_z(d), l).start()
     for d in range(1, nz):
         stage1(d).start()
-    for t in qry_peers:
-        remote(pack, atoms_in.at[q, l], send_a, recv_a, t, l).start()
-    for tq, tl in peers:
-        remote(codes_out.at[tl * nq + tq], codes_in.at[me], send_c, recv_c, tq, tl).start()
     for k in range(nl):
         gath[k, pl.ds(pl.multiple_of(q * block, block), block), :] = qp_ref[:, k * cols : (k + 1) * cols]
     for k in range(nl):
         to_sib(q, k).start()
-    atoms_in[q, l] = pack[...]
-    codes_in[me] = codes_out[me_o]
+    atoms_in[l, c, z] = pack[...]
 
     conf_copy.wait()
     comps = prepare(*(conf[i * atoms : (i + 1) * atoms] for i in range(4)))
@@ -253,21 +257,29 @@
         cself[0:1, lanes] = self_overlap(confp, lanes, atoms)
         return carry
 
-    lax.fori_loop(0, own_rows // LANES, self_step, 0)
-
-    q_rest = pl.ds(0, nq - 1)
+    selves = own_rows // LANES
+    lax.fori_loop(0, selves // 3, self_step, 0)
+
+    pl.semaphore_wait(ready, nl - 1)
+    for tq, tl in peers:
+        remote(codes_out.at[tl * nq + tq], codes_in.at[me], send_c, recv_c, tq, tl).start()
+    codes_in[me] = codes_out[me_o]
+
+    lax.fori_loop(selves // 3, selves, self_step, 0)
+
+    z_rest = pl.ds(0, nz - 1)
     l_rest = pl.ds(0, nl - 1)
     d_rest = pl.ds(0, dev - 1)
 
+    take(atoms_in.at[0, 0, z_rest], recv_a)
+    for e in range(nl - 1, 0, -1):
+        atoms_to(l, q, flip(l, e), send_b, recv_b).start()
+    atoms_to(l, sib, l, send_e, recv_e).start()
     for d in range(1, nz):
         stage1(d).wait_recv()
         for e in range(nl - 1, 0, -1):
             stage2(d, e).start()
         to_sib(from_z(d), l).start()
-        if d == 1:
-            take(atoms_in.at[q_rest, 0], recv_a)
-            for t in lib_peers:
-                remote(atoms_in.at[:, l], atoms_in.at[:, l], send_b, recv_b, q, t).start()
 
     take(codes_in.at[d_rest], recv_c)
     parts = [None] * groups
@@ -282,15 +294,23 @@
     valid = pcode > 0
     pcode = jnp.maximum(pcode - 1, 0)
     pslot = fdiv(pcode, local_q)
-    pquery = fdiv(iota((1, pairs), 1), cap) * local_q + (pcode - pslot * local_q)
+    source = fdiv(iota((1, pairs), 1), cap)
+    which = pcode - pslot * local_q
+    pquery = source * local_q + which
+    src_q, src_l = source // nl, source % nl
+    held = ((src_l * CORES + src_q % CORES) * nz + src_q // CORES) * local_q + which
     onehot[...] = jnp.where(iota((own_rows, pairs), 0) == pslot, 1.0, 0.0).astype(BF16)
-    qonehot[...] = jnp.where(iota((dev * local_q, pairs), 0) == pquery, 1.0, 0.0).astype(BF16)
+    qonehot[...] = jnp.where(iota((dev * local_q, pairs), 0) == held, 1.0, 0.0).astype(BF16)
+
+    take(atoms_in.at[l_rest, 0], recv_b)
+    for e in range(nl - 1, 0, -1):
+        atoms_to(flip(l, e), sib, l, send_e, recv_e).start()
 
     pad = jnp.zeros((7, own_rows), F32)
     hi_c, lo_c = split2(jnp.concatenate([confp[...], cself[...], pad], axis=0))
     pairs_c[...] = nn(hi_c, onehot[...]) + nn(lo_c, onehot[...])
 
-    take(atoms_in.at[:, l_rest], recv_b)
+    take(atoms_in.at[:, 0], recv_e)
     raw = atoms_in[...].reshape(dev, 2 * local_q, LANES).astype(F32)
     q_top = jnp.transpose(raw[:, :local_q].reshape(dev * local_q, LANES))
     q_low = jnp.transpose(raw[:, local_q:].reshape(dev * local_q, LANES))
@@ -303,7 +323,7 @@
     pairs_q[...] = nn(hi_q, qonehot[...]) + nn(lo_q, qonehot[...])
 
     n_far = (nz - 1) * (nl - 1)
-    each = (n_far + groups - 1) // groups
+    each = (2 * n_far + groups - 1) // groups
 
     def onward(n):
         d = 1 + lax.div(n, nl - 1)
@@ -363,8 +383,9 @@
     take(gath.at[0, pl.ds(0, (nz - 1) * block), :], s1_send)
     take(gath.at[pl.ds(0, nl - 1), pl.ds(0, (nz - 1) * block), :], s2_send)
     take(gath.at[:, pl.ds(0, nz * block), :], sib_send)
-    take(atoms_in.at[q_rest, 0], send_a)
-    take(atoms_in.at[:, l_rest], send_b)
+    take(atoms_in.at[0, 0, z_rest], send_a)
+    take(atoms_in.at[l_rest, 0], send_b)
+    take(atoms_in.at[:, 0], send_e)
     take(codes_in.at[d_rest], send_c)
     tv_copy.wait()
     take(ret_in.at[d_rest], recv_d)
@@ -437,7 +458,7 @@
             vm((4 * atoms, own_rows), F32),
             vm((nl, rows, width // nl), BF16),
             vm((2 * local_q, LANES), BF16),
-            vm((nq, nl, 2 * local_q, LANES), BF16),
+            vm((nl, CORES, nz, 2 * local_q, LANES), BF16),
             vm((dev, 2, 1, LANES), I32),
             vm((dev, 2, 1, LANES), I32),
             vm((pairs // LANES + 1, 1, LANES), F32),
@@ -455,7 +476,8 @@
             dma, dma((nz,)),
             dma, dma,
             dma, dma((nz, nl)),
-            dma, dma, dma, dma, dma, dma, dma, dma,
+            dma, dma, dma, dma, dma, dma, dma, dma, dma, dma,
+            pltpu.SemaphoreType.REGULAR,
         ],
         compiler_params=pltpu.CompilerParams(
             collective_id=0, has_side_effects=True, vmem_limit_bytes=limit

time: 31.9 us -> 28.2 us (0.88)
  Pallas kernels: 31.1 us -> 27.3 us
    pallas_call x1, Pallas kernels: 29.3 us -> 25.6 us  [body(): pl.pallas_call(functools.partial(kernel, nq, nl, cap, id_bytes), out_shap...]
where the time goes in v2:
time: 28.2 us; the launch traced here: 28 us
  Pallas kernels  27.3 us (97%)
  between operations  0.64 us (2%)
    pallas_call x1, Pallas kernels, body(): pl.pallas_call(functools.partial(kernel, nq, nl, cap, id_bytes), out_shap...  25.6 us
    pallas_call x1, Pallas kernels, hand_over(): pl.pallas_call(copy_out, out_shape=(jax.ShapeDtypeStruct(tv.shape, tv.dty...  1.76 us

profile of v2, /device:TPU:0, one launch (start us, length us, event | category | flops | bytes accessed | tf_op | source)
XLA Modules:
  0.0 28.0 jit_solution(16838371646822776797)
XLA Ops:
  0.6 25.6 %shard_map.86 = (bf16[256,768]{1,0:T(8,128)(2,1)}, f32[8,64]{1,0:T(8,128)}) custom-call(bf16[32,2048]{1,0:T(8,128)(2,1)} %qp_hbm.1, bf16[768,2048]{1,0:T(8,128)(2,1)} %lib_hbm.1, f32[8,192]{1,0:T(8,128)} %qa_hbm.1, f32[192,768]{1,0:T(8,128)} %bitcast.2, s32[8,64]{1,0:T(8,128)} %cand_hbm.1, s32[8]{0:T(128)} %count_hbm.1, s32[192,128]{1,0:T(8,128)} %bitcast.3), custom_call_target="tpu_custom_call" | custom-call | tf_op jit(solution)/shard_map/pallas_call | solution.py:442
  26.2 1.8 %shard_map.87 = (bf16[256,768]{1,0:T(8,128)(2,1)}, f32[8,64]{1,0:T(8,128)}) custom-call(bf16[256,768]{1,0:T(8,128)(2,1)} %get-tuple-element.4.tv_in, f32[8,64]{1,0:T(8,128)} %get-tuple-element.5.score_in), custom_call_target="tpu_custom_call" | custom-call | tf_op jit(solution)/shard_map/pallas_call | solution.py:417

commit v3 on v2

--- a/solution.py
+++ b/solution.py
@@ -92,12 +92,12 @@
 
 def kernel(
     nq, nl, cap, id_bytes,
-    qp_hbm, lib_hbm, qa_hbm, conf_hbm, cand_hbm, count_hbm, home_hbm,
-    tv_hbm, out_ref,
+    qp_hbm, lib_hbm, qa_hbm, conf_hbm, cand_hbm, home_hbm,
+    tv_hbm, ret_in, meta_hbm,
     tv_ref,
-    qp_ref, qa_ref, cand_ref, count_ref, home_ref,
-    lib, conf, gath, pack, atoms_in, codes_out, codes_in, score, ret_in,
-    confp, qprep, ownprep, pairs_c, pairs_q, onehot, qonehot, cself, shape_s,
+    qp_ref, qa_ref, cand_ref, home_ref,
+    lib, turned, conf, gath, pack, atoms_in, codes_out, codes_in, score, meta,
+    confp, qprep, ownprep, pairs_c, pairs_q, inv_ref, onehot, qonehot, cself, shape_s,
     loc_sem, s1_send, s1_recv, sib_send, sib_recv, s2_send, s2_recv,
     send_a, recv_a, send_b, recv_b, send_c, recv_c, send_d, recv_d, send_e, recv_e, ready,
 ):
@@ -137,7 +137,7 @@
     loads = [
         pltpu.make_async_copy(src, dst, loc_sem.at[2 + n])
         for n, (src, dst) in enumerate(
-            ((qa_hbm, qa_ref), (cand_hbm, cand_ref), (home_hbm, home_ref), (qp_hbm, qp_ref), (count_hbm, count_ref))
+            ((qa_hbm, qa_ref), (cand_hbm, cand_ref), (home_hbm, home_ref), (qp_hbm, qp_ref))
         )
     ]
     for load in loads:
@@ -152,41 +152,8 @@
             barrier, inc=1, device_id={"qry": tq, "lib": tl}, device_id_type=pl.DeviceIdType.MESH
         )
 
-    for load in loads:
-        load.wait()
-
-    ids = jnp.concatenate([cand_ref[pl.ds(i, 1), :] for i in range(local_q)], axis=1)
-    table = home_ref[...]
-    trows = table.shape[0]
-    pieces = [
-        jnp.transpose(((table >> (8 * k)) & 255).astype(F32)).astype(BF16) for k in range(id_bytes)
-    ]
-    row_hot = jnp.where(iota((trows, cand_n), 0) == (ids >> 7), 1.0, 0.0).astype(BF16)
-    lane_hot = iota((LANES, cand_n), 0) == (ids & 127)
-    stored = jnp.zeros((1, cand_n), I32)
-    for k in range(id_bytes):
-        found = nn(pieces[k], row_hot)
-        byte = jnp.sum(jnp.where(lane_hot, found, 0.0), axis=0, keepdims=True)
-        stored = stored + (byte.astype(I32) << (8 * k))
-    owner = fdiv(stored, own_rows)
-    slot = stored - owner * own_rows
-
-    owns = iota((dev, cand_n), 0) == owner
-    owns_b = jnp.where(owns, 1.0, 0.0).astype(BF16)
-    tri = jnp.where(iota((cand_n, cand_n), 0) < iota((cand_n, cand_n), 1), 1.0, 0.0).astype(BF16)
-    before = nn(owns_b, tri)
-    rank = jnp.sum(jnp.where(owns, before, 0.0), axis=0, keepdims=True).astype(I32)
-    my_off = lax.rem(cap * me, LANES)
-    rank_b = jnp.where(iota((2 * LANES, cand_n), 0) == rank + my_off, 1.0, 0.0).astype(BF16)
-    code = slot * local_q + fdiv(iota((1, cand_n), 1), listed) + 1
-    lo = (code & 127).astype(F32)
-    hi = (code >> 7).astype(F32)
-    left = jnp.concatenate([jnp.where(owns, lo, 0.0), jnp.where(owns, hi, 0.0)], axis=0).astype(BF16)
-    sums = nt(left, rank_b).astype(I32)
-    codes = sums[:dev] + (sums[dev:] << 7)
-    for o in range(dev):
-        for k in range(2):
-            codes_out[o, k] = codes[o : o + 1, k * LANES : (k + 1) * LANES]
+    loads[3].wait()
+    loads[0].wait()
 
     qa = qa_ref[...]
     zero = jnp.zeros((local_q, LANES - half), F32)
@@ -204,7 +171,16 @@
         jnp.where(lane_at == iota((local_q, LANES), 0), own_self, 0.0), axis=1, keepdims=True
     )
     own_hi = own_col.astype(BF16).astype(F32)
-    low = jnp.where(lane_at == half, own_hi, jnp.where(lane_at == half + 1, own_col - own_hi, low))
+    prints = qp_ref[...].astype(F32)
+    squares = jnp.sum(prints * prints, axis=1, keepdims=True)
+    norm = jnp.zeros((local_q, 1), F32)
+    for k in range(nl):
+        norm = norm + jnp.where(l == k, squares[k * local_q : (k + 1) * local_q], 0.0)
+    norm_hi = norm.astype(BF16).astype(F32)
+    norm_mid = (norm - norm_hi).astype(BF16).astype(F32)
+    extra = (own_hi, own_col - own_hi, norm_hi, norm_mid, norm - norm_hi - norm_mid)
+    for k, column in enumerate(extra):
+        low = jnp.where(lane_at == half + k, column, low)
     pack[...] = jnp.concatenate([top, low], axis=0).astype(BF16)
 
     pl.semaphore_wait(barrier, nq + nl - 2)
@@ -247,6 +223,51 @@
         to_sib(q, k).start()
     atoms_in[l, c, z] = pack[...]
 
+    for load in loads[1:3]:
+        load.wait()
+
+    ids = jnp.concatenate([cand_ref[pl.ds(i, 1), :] for i in range(local_q)], axis=1)
+    table = home_ref[...]
+    trows = table.shape[0]
+    pieces = [
+        jnp.transpose(((table >> (8 * k)) & 255).astype(F32)).astype(BF16) for k in range(id_bytes)
+    ]
+    row_hot = jnp.where(iota((trows, cand_n), 0) == (ids >> 7), 1.0, 0.0).astype(BF16)
+    lane_hot = iota((LANES, cand_n), 0) == (ids & 127)
+    stored = jnp.zeros((1, cand_n), I32)
+    for k in range(id_bytes):
+        found = nn(pieces[k], row_hot)
+        byte = jnp.sum(jnp.where(lane_hot, found, 0.0), axis=0, keepdims=True)
+        stored = stored + (byte.astype(I32) << (8 * k))
+    owner = fdiv(stored, own_rows)
+    slot = stored - owner * own_rows
+
+    owns = iota((dev, cand_n), 0) == owner
+    owns_b = jnp.where(owns, 1.0, 0.0).astype(BF16)
+    tri = jnp.where(iota((cand_n, cand_n), 0) < iota((cand_n, cand_n), 1), 1.0, 0.0).astype(BF16)
+    before = nn(owns_b, tri)
+    rank = jnp.sum(jnp.where(owns, before, 0.0), axis=0, keepdims=True).astype(I32)
+    my_off = lax.rem(cap * me, LANES)
+    meta[0] = owner
+    meta[1] = rank + my_off
+    meta_copy = pltpu.make_async_copy(meta, meta_hbm, loc_sem.at[6])
+    meta_copy.start()
+    rank_b = jnp.where(iota((2 * LANES, cand_n), 0) == rank + my_off, 1.0, 0.0).astype(BF16)
+    code = slot * local_q + fdiv(iota((1, cand_n), 1), listed) + 1
+    lo = (code & 127).astype(F32)
+    hi = (code >> 7).astype(F32)
+    left = jnp.concatenate([jnp.where(owns, lo, 0.0), jnp.where(owns, hi, 0.0)], axis=0).astype(BF16)
+    sums = nt(left, rank_b).astype(I32)
+    codes = sums[:dev] + (sums[dev:] << 7)
+    for o in range(dev):
+        for k in range(2):
+            codes_out[o, k] = codes[o : o + 1, k * LANES : (k + 1) * LANES]
+
+    pl.semaphore_wait(ready, nl - 1)
+    for tq, tl in peers:
+        remote(codes_out.at[tl * nq + tq], codes_in.at[me], send_c, recv_c, tq, tl).start()
+    codes_in[me] = codes_out[me_o]
+
     conf_copy.wait()
     comps = prepare(*(conf[i * atoms : (i + 1) * atoms] for i in range(4)))
     for i in range(4):
@@ -258,19 +279,22 @@
         return carry
 
     selves = own_rows // LANES
-    lax.fori_loop(0, selves // 3, self_step, 0)
-
-    pl.semaphore_wait(ready, nl - 1)
-    for tq, tl in peers:
-        remote(codes_out.at[tl * nq + tq], codes_in.at[me], send_c, recv_c, tq, tl).start()
-    codes_in[me] = codes_out[me_o]
-
-    lax.fori_loop(selves // 3, selves, self_step, 0)
+    lax.fori_loop(0, selves, self_step, 0)
 
     z_rest = pl.ds(0, nz - 1)
     l_rest = pl.ds(0, nl - 1)
     d_rest = pl.ds(0, dev - 1)
 
+    lib_copy.wait()
+    blocks = own_rows // LANES
+    turns = [n * blocks // nz for n in range(nz + 1)]
+
+    def turn(n):
+        for b in range(turns[n], turns[n + 1]):
+            at = slice(b * LANES, (b + 1) * LANES)
+            turned[:, at] = jnp.transpose(lib[at, :])
+
+    turn(0)
     take(atoms_in.at[0, 0, z_rest], recv_a)
     for e in range(nl - 1, 0, -1):
         atoms_to(l, q, flip(l, e), send_b, recv_b).start()
@@ -280,6 +304,7 @@
         for e in range(nl - 1, 0, -1):
             stage2(d, e).start()
         to_sib(from_z(d), l).start()
+        turn(d)
 
     take(codes_in.at[d_rest], recv_c)
     parts = [None] * groups
@@ -306,9 +331,13 @@
     for e in range(nl - 1, 0, -1):
         atoms_to(flip(l, e), sib, l, send_e, recv_e).start()
 
-    pad = jnp.zeros((7, own_rows), F32)
-    hi_c, lo_c = split2(jnp.concatenate([confp[...], cself[...], pad], axis=0))
-    pairs_c[...] = nn(hi_c, onehot[...]) + nn(lo_c, onehot[...])
+    self_hi, self_lo = split2(cself[...])
+    pad = jnp.zeros((14, own_rows), BF16)
+    found = nn(jnp.concatenate([conf[...].astype(BF16), self_hi, self_lo, pad], axis=0), onehot[...])
+    comps = prepare(*(found[i * atoms : (i + 1) * atoms] for i in range(4)))
+    for i in range(4):
+        pairs_c[i * atoms : (i + 1) * atoms] = comps[i]
+    pairs_c[4 * atoms : 4 * atoms + 1] = found[4 * atoms : 4 * atoms + 1] + found[4 * atoms + 1 : 4 * atoms + 2]
 
     take(atoms_in.at[:, 0], recv_e)
     raw = atoms_in[...].reshape(dev, 2 * local_q, LANES).astype(F32)
@@ -321,6 +350,11 @@
     pad = jnp.zeros((7, dev * local_q), F32)
     hi_q, lo_q = split2(jnp.concatenate([qprep[...], qself, pad], axis=0))
     pairs_q[...] = nn(hi_q, qonehot[...]) + nn(lo_q, qonehot[...])
+    inverse = raw[:, local_q:, half + 2 : half + 3] + raw[:, local_q:, half + 3 : half + 4]
+    inverse = 1.0 / (inverse + raw[:, local_q:, half + 4 : half + 5] + EPSILON)
+    for s in range(dev):
+        there = (s % nl * CORES + s // nl % CORES) * nz + s // nl // CORES
+        inv_ref[s * local_q : (s + 1) * local_q, :] = inverse[there]
 
     n_far = (nz - 1) * (nl - 1)
     each = (2 * n_far + groups - 1) // groups
@@ -347,21 +381,16 @@
     lax.fori_loop(0, groups, cross_step, 0)
 
     take(gath.at[:, pl.ds(0, nz * block), :], sib_recv)
-    lib_copy.wait()
 
     rows = nq * block
     chunk = min(rows, 256)
     for r in range(0, rows, chunk):
         scores = None
-        norms = None
         for k in range(nl):
             part = gath[k, r : r + chunk, :]
-            prod = nt(part, lib[:, k * cols : (k + 1) * cols])
-            wide = part.astype(F32)
-            sq = jnp.sum(wide * wide, axis=1, keepdims=True)
+            prod = nn(part, turned[k * cols : (k + 1) * cols, :])
             scores = prod if scores is None else scores + prod
-            norms = sq if norms is None else norms + sq
-        tv_ref[r : r + chunk, :] = (scores * (1.0 / (norms + EPSILON))).astype(BF16)
+        tv_ref[r : r + chunk, :] = (scores * inv_ref[r : r + chunk, :]).astype(BF16)
 
     tv_copy = pltpu.make_async_copy(tv_ref, tv_hbm, loc_sem.at[7])
     tv_copy.start()
@@ -378,7 +407,8 @@
     for tq, tl in peers:
         at = lax.div(cap * (tq * nl + tl), LANES)
         remote(score.at[pl.ds(at, 2)], ret_in.at[me_o], send_d, recv_d, tq, tl).start()
-    ret_in[me_o] = score[pl.ds(lax.div(cap * me, LANES), 2)]
+    own_copy = pltpu.make_async_copy(score.at[pl.ds(lax.div(cap * me, LANES), 2)], ret_in.at[me_o], loc_sem.at[5])
+    own_copy.start()
 
     take(gath.at[0, pl.ds(0, (nz - 1) * block), :], s1_send)
     take(gath.at[pl.ds(0, nl - 1), pl.ds(0, (nz - 1) * block), :], s2_send)
@@ -388,39 +418,40 @@
     take(atoms_in.at[:, 0], send_e)
     take(codes_in.at[d_rest], send_c)
     tv_copy.wait()
+    meta_copy.wait()
+    own_copy.wait()
     take(ret_in.at[d_rest], recv_d)
-
+    take(ret_in.at[d_rest], send_d)
+
+
+def finish(tv_in, ret_in, meta, count, tv_out, out_ref, sem):
+    copy = pltpu.make_async_copy(tv_in, tv_out, sem)
+    copy.start()
+    dev = ret_in.shape[0]
+    local_q, listed = out_ref.shape
+    cand_n = local_q * listed
+    owns = iota((dev, cand_n), 0) == meta[0]
+    rank_b = jnp.where(iota((2 * LANES, cand_n), 0) == meta[1], 1.0, 0.0).astype(BF16)
     came = jnp.concatenate([ret_in[:, k].reshape(dev, LANES) for k in range(2)], axis=1)
     hi_b, lo_b = split2(came)
     mine = nn(hi_b, rank_b) + nn(lo_b, rank_b)
     final = jnp.sum(jnp.where(owns, mine, 0.0), axis=0, keepdims=True)
     for i in range(local_q):
         line = final[:, i * listed : (i + 1) * listed]
-        live = iota((1, listed), 1) < count_ref[i]
+        live = iota((1, listed), 1) < count[i]
         out_ref[i : i + 1, :] = jnp.where(live, line, 0.0)
-
-    take(ret_in.at[d_rest], send_d)
-
-
-def copy_out(tv_in, score_in, tv_out, score_out, sems):
-    copies = [
-        pltpu.make_async_copy(tv_in, tv_out, sems.at[0]),
-        pltpu.make_async_copy(score_in, score_out, sems.at[1]),
-    ]
-    for copy in copies:
-        copy.start()
-    for copy in copies:
-        copy.wait()
-
-
-def hand_over(tv, score):
+    copy.wait()
+
+
+def hand_over(tv, ret, meta, count, out_shape):
+    vspec = pl.BlockSpec(memory_space=pltpu.VMEM)
     return pl.pallas_call(
-        copy_out,
-        out_shape=(jax.ShapeDtypeStruct(tv.shape, tv.dtype), jax.ShapeDtypeStruct(score.shape, score.dtype)),
-        in_specs=[pl.BlockSpec(memory_space=pltpu.VMEM)] * 2,
-        out_specs=(pl.BlockSpec(memory_space=pl.ANY), pl.BlockSpec(memory_space=pl.ANY)),
-        scratch_shapes=[pltpu.SemaphoreType.DMA((2,))],
-    )(tv, score)
+        finish,
+        out_shape=(jax.ShapeDtypeStruct(tv.shape, tv.dtype), jax.ShapeDtypeStruct(out_shape, F32)),
+        in_specs=[vspec, vspec, vspec, pl.BlockSpec(memory_space=pltpu.SMEM)],
+        out_specs=(pl.BlockSpec(memory_space=pl.ANY), vspec),
+        scratch_shapes=[pltpu.SemaphoreType.DMA],
+    )(tv, ret, meta, count)
 
 
 def body(nq, nl, query_prints, library_prints, query_atoms, conformer_atoms, candidates, candidate_count, home_row):
@@ -438,23 +469,24 @@
     limit = 56 * 1024 * 1024
     vm = pltpu.VMEM
     dma = pltpu.SemaphoreType.DMA
-    vspec = pl.BlockSpec(memory_space=pltpu.VMEM)
-    tv, score = pl.pallas_call(
+    hspec = pl.BlockSpec(memory_space=pl.ANY)
+    tv, ret, meta = pl.pallas_call(
         functools.partial(kernel, nq, nl, cap, id_bytes),
         out_shape=(
             jax.ShapeDtypeStruct((rows, own_rows), BF16),
-            jax.ShapeDtypeStruct((local_q, listed), F32),
+            jax.ShapeDtypeStruct((dev, 2, 1, LANES), F32),
+            jax.ShapeDtypeStruct((2, 1, cand_n), I32),
         ),
-        in_specs=[pl.BlockSpec(memory_space=pltpu.HBM)] * 7,
-        out_specs=(pl.BlockSpec(memory_space=pl.ANY), vspec),
+        in_specs=[pl.BlockSpec(memory_space=pltpu.HBM)] * 6,
+        out_specs=(hspec, hspec, hspec),
         scratch_shapes=[
             vm((rows, own_rows), BF16),
             vm((block, width), BF16),
             vm((local_q, 4 * atoms), F32),
             vm((local_q, listed), I32),
-            pltpu.SMEM((local_q,), I32),
             vm((home_row.shape[0] // LANES, LANES), I32),
             vm((own_rows, width), BF16),
+            vm((width, own_rows), BF16),
             vm((4 * atoms, own_rows), F32),
             vm((nl, rows, width // nl), BF16),
             vm((2 * local_q, LANES), BF16),
@@ -462,12 +494,13 @@
             vm((dev, 2, 1, LANES), I32),
             vm((dev, 2, 1, LANES), I32),
             vm((pairs // LANES + 1, 1, LANES), F32),
-            vm((dev, 2, 1, LANES), F32),
+            vm((2, 1, cand_n), I32),
             vm((4 * atoms, own_rows), F32),
             vm((4 * atoms, rows), F32),
             vm((4 * atoms, LANES), F32),
             vm((4 * atoms + 8, pairs), F32),
             vm((4 * atoms + 8, pairs), F32),
+            vm((rows, 1), F32),
             vm((own_rows, pairs), BF16),
             vm((rows, pairs), BF16),
             vm((1, own_rows), F32),
@@ -483,10 +516,10 @@
             collective_id=0, has_side_effects=True, vmem_limit_bytes=limit
         ),
     )(
-        query_prints, library_prints, query_atoms, conformer_atoms.T, candidates, candidate_count,
+        query_prints, library_prints, query_atoms, conformer_atoms.T, candidates,
         home_row.reshape(-1, LANES),
     )
-    return hand_over(tv, score)
+    return hand_over(tv, ret, meta, candidate_count, (local_q, listed))
 
 
 def solution(mesh):

time: 28.2 us -> 27.6 us (0.979)
  Pallas kernels: 27.3 us -> 26.8 us
    pallas_call x1, Pallas kernels: 25.6 us -> 24.4 us  [body(): pl.pallas_call(functools.partial(kernel, nq, nl, cap, id_bytes), out_shap...]
    pallas_call x1, Pallas kernels: 1.76 us -> 2.37 us  [hand_over(): pl.pallas_call(finish, out_shape=(jax.ShapeDtypeStruct(tv.shape, tv.dtype...]
where the time goes in v3:
time: 27.6 us; the launch traced here: 27.4 us
  Pallas kernels  26.8 us (97%)
  between operations  0.64 us (2%)
    pallas_call x1, Pallas kernels, body(): pl.pallas_call(functools.partial(kernel, nq, nl, cap, id_bytes), out_shap...  24.4 us
    pallas_call x1, Pallas kernels, hand_over(): pl.pallas_call(finish, out_shape=(jax.ShapeDtypeStruct(tv.shape, tv.dtype...  2.37 us

profile of v3, /device:TPU:0, one launch (start us, length us, event | category | flops | bytes accessed | tf_op | source)
XLA Modules:
  0.0 27.4 jit_solution(4685500609359650969)
XLA Ops:
  0.6 24.4 %shard_map.86 = (bf16[256,768]{1,0:T(8,128)(2,1)}, f32[32,2,1,128]{3,2,1,0:T(1,128)}, s32[2,1,512]{2,1,0:T(1,128)}) custom-call(bf16[32,2048]{1,0:T(8,128)(2,1)} %qp_hbm.1, bf16[768,2048]{1,0:T(8,128)(2,1)} %lib_hbm.1, f32[8,192]{1,0:T(8,128)} %qa_hbm.1, f32[192,768]{1,0:T(8,128)} %bitcast.2, s32[8,64]{1,0:T(8,128)} %cand_hbm.1, s32[192,128]{1,0:T(8,128)} %bitcast.3), custom_call_target="tpu_custom_call" | custom-call | tf_op jit(solution)/shard_map/pallas_call | solution.py:473
  25.1 2.4 %shard_map.87 = (bf16[256,768]{1,0:T(8,128)(2,1)}, f32[8,64]{1,0:T(8,128)}) custom-call(bf16[256,768]{1,0:T(8,128)(2,1)} %get-tuple-element.5.tv_in, f32[32,2,1,128]{3,2,1,0:T(1,128)} %get-tuple-element.6.ret_in, s32[2,1,512]{2,1,0:T(1,128)} %get-tuple-element.7.meta, s32[8]{0:T(128)} %count.1), custom_call_target="tpu_custom_call" | custom-call | tf_op jit(solution)/shard_map/pallas_call | solution.py:448

commit v4 on v3

--- a/solution.py
+++ b/solution.py
@@ -97,7 +97,7 @@
     tv_ref,
     qp_ref, qa_ref, cand_ref, home_ref,
     lib, turned, conf, gath, pack, atoms_in, codes_out, codes_in, score, meta,
-    confp, qprep, ownprep, pairs_c, pairs_q, inv_ref, onehot, qonehot, cself, shape_s,
+    confp, ownprep, pairs_c, pairs_q, inv_ref, onehot, qonehot, cself, shape_s,
     loc_sem, s1_send, s1_recv, sib_send, sib_recv, s2_send, s2_recv,
     send_a, recv_a, send_b, recv_b, send_c, recv_c, send_d, recv_d, send_e, recv_e, ready,
 ):
@@ -205,9 +205,9 @@
         there = piece(from_z(d), l)
         return remote(there, there, s2_send, s2_recv.at[d, e], q, flip(l, e))
 
-    def to_sib(bq, k):
+    def to_sib(bq, k, late):
         there = piece(bq, k)
-        return remote(there, there, sib_send, sib_recv, sib, l)
+        return remote(there, there, sib_send, sib_recv.at[late], sib, l)
 
     def atoms_to(k, dq, dl, ssem, rsem):
         there = atoms_in.at[k, c]
@@ -219,8 +219,6 @@
         stage1(d).start()
     for k in range(nl):
         gath[k, pl.ds(pl.multiple_of(q * block, block), block), :] = qp_ref[:, k * cols : (k + 1) * cols]
-    for k in range(nl):
-        to_sib(q, k).start()
     atoms_in[l, c, z] = pack[...]
 
     for load in loads[1:3]:
@@ -266,6 +264,8 @@
     pl.semaphore_wait(ready, nl - 1)
     for tq, tl in peers:
         remote(codes_out.at[tl * nq + tq], codes_in.at[me], send_c, recv_c, tq, tl).start()
+    for k in range(nl):
+        to_sib(q, k, 0).start()
     codes_in[me] = codes_out[me_o]
 
     conf_copy.wait()
@@ -303,7 +303,7 @@
         stage1(d).wait_recv()
         for e in range(nl - 1, 0, -1):
             stage2(d, e).start()
-        to_sib(from_z(d), l).start()
+        to_sib(from_z(d), l, 0 if d < nz // 2 else 1).start()
         turn(d)
 
     take(codes_in.at[d_rest], recv_c)
@@ -343,54 +343,68 @@
     raw = atoms_in[...].reshape(dev, 2 * local_q, LANES).astype(F32)
     q_top = jnp.transpose(raw[:, :local_q].reshape(dev * local_q, LANES))
     q_low = jnp.transpose(raw[:, local_q:].reshape(dev * local_q, LANES))
-    comps = prepare(q_top[:atoms], q_top[atoms:half], q_low[:atoms], q_low[atoms:half])
+    found = nn(jnp.concatenate([q_top, q_low], axis=0).astype(BF16), qonehot[...])
+    comps = prepare(
+        found[:atoms], found[atoms:half], found[LANES : LANES + atoms], found[LANES + atoms : LANES + half]
+    )
     for i in range(4):
-        qprep[i * atoms : (i + 1) * atoms] = comps[i]
-    qself = q_low[half : half + 1] + q_low[half + 1 : half + 2]
-    pad = jnp.zeros((7, dev * local_q), F32)
-    hi_q, lo_q = split2(jnp.concatenate([qprep[...], qself, pad], axis=0))
-    pairs_q[...] = nn(hi_q, qonehot[...]) + nn(lo_q, qonehot[...])
+        pairs_q[i * atoms : (i + 1) * atoms] = comps[i]
+    own = LANES + half
+    pairs_q[4 * atoms : 4 * atoms + 1] = found[own : own + 1] + found[own + 1 : own + 2]
     inverse = raw[:, local_q:, half + 2 : half + 3] + raw[:, local_q:, half + 3 : half + 4]
     inverse = 1.0 / (inverse + raw[:, local_q:, half + 4 : half + 5] + EPSILON)
     for s in range(dev):
         there = (s % nl * CORES + s // nl % CORES) * nz + s // nl // CORES
         inv_ref[s * local_q : (s + 1) * local_q, :] = inverse[there]
 
-    n_far = (nz - 1) * (nl - 1)
-    each = (2 * n_far + groups - 1) // groups
-
-    def onward(n):
+    def onward(late, n):
         d = 1 + lax.div(n, nl - 1)
         e = nl - 1 - lax.rem(n, nl - 1)
         stage2(d, e).wait_recv()
-        to_sib(from_z(d), flip(l, e)).start()
-
-    def cross_step(g, carry):
+        to_sib(from_z(d), flip(l, e), late).start()
+
+    def cross_step(late, first, last, start, each, g, carry):
         for k in range(each):
-            n = g * each + k
-            if groups * each == n_far:
-                onward(n)
+            n = first + (g - start) * each + k
+            if (last - first) % each:
+                pl.when(n < last)(functools.partial(onward, late, n))
             else:
-                pl.when(n < n_far)(functools.partial(onward, n))
+                onward(late, n)
         lanes = pl.ds(pl.multiple_of(g * LANES, LANES), LANES)
         cross = cross_overlap(pairs_q, pairs_c, lanes, atoms)
         selves = pairs_q[4 * atoms : 4 * atoms + 1, lanes] + pairs_c[4 * atoms : 4 * atoms + 1, lanes]
         shape_s[0:1, lanes] = cross / (selves - cross)
         return carry
 
-    lax.fori_loop(0, groups, cross_step, 0)
-
-    take(gath.at[:, pl.ds(0, nz * block), :], sib_recv)
+    def cross_groups(late, first, last, start, stop):
+        each = (last - first + stop - start - 1) // (stop - start)
+        stop_at = stop if each == 0 else start + (last - first + each - 1) // each
+        step = functools.partial(cross_step, late, first, last, start, each)
+        lax.fori_loop(start, stop_at, step, 0)
+        if stop_at < stop:
+            lax.fori_loop(stop_at, stop, functools.partial(cross_step, late, last, last, start, 0), 0)
 
     rows = nq * block
     chunk = min(rows, 256)
+
+    n_near, n_far = (nz // 2 - 1) * (nl - 1), (nz - 1) * (nl - 1)
+    cuts = (groups // 3, 2 * groups // 3)
+    cross_groups(0, 0, n_near, 0, cuts[0])
+    cross_groups(1, n_near, n_far, cuts[0], cuts[1])
+
+    part_prints = gath.at[:, pl.ds(0, nz * block // 2), :]
+
+    cross_groups(1, n_far, n_far, cuts[1], groups)
+
+    take(part_prints, sib_recv.at[0])
+    take(part_prints, sib_recv.at[1])
     for r in range(0, rows, chunk):
+        at = slice(r, r + chunk)
         scores = None
         for k in range(nl):
-            part = gath[k, r : r + chunk, :]
-            prod = nn(part, turned[k * cols : (k + 1) * cols, :])
+            prod = nn(gath[k, at, :], turned[k * cols : (k + 1) * cols, :])
             scores = prod if scores is None else scores + prod
-        tv_ref[r : r + chunk, :] = (scores * inv_ref[r : r + chunk, :]).astype(BF16)
+        tv_ref[at, :] = (scores * inv_ref[at, :]).astype(BF16)
 
     tv_copy = pltpu.make_async_copy(tv_ref, tv_hbm, loc_sem.at[7])
     tv_copy.start()
@@ -496,7 +510,6 @@
             vm((pairs // LANES + 1, 1, LANES), F32),
             vm((2, 1, cand_n), I32),
             vm((4 * atoms, own_rows), F32),
-            vm((4 * atoms, rows), F32),
             vm((4 * atoms, LANES), F32),
             vm((4 * atoms + 8, pairs), F32),
             vm((4 * atoms + 8, pairs), F32),
@@ -507,7 +520,7 @@
             vm((1, pairs), F32),
             dma((8,)),
             dma, dma((nz,)),
-            dma, dma,
+            dma, dma((2,)),
             dma, dma((nz, nl)),
             dma, dma, dma, dma, dma, dma, dma, dma, dma, dma,
             pltpu.SemaphoreType.REGULAR,

time: 27.6 us -> 27.3 us (0.989)
  Pallas kernels: 26.8 us -> 26.5 us
    pallas_call x1, Pallas kernels: 24.4 us -> 24.1 us  [body(): pl.pallas_call(functools.partial(kernel, nq, nl, cap, id_bytes), out_shap...]
where the time goes in v4:
time: 27.3 us; the launch traced here: 27.1 us
  Pallas kernels  26.5 us (97%)
  between operations  0.64 us (2%)
    pallas_call x1, Pallas kernels, body(): pl.pallas_call(functools.partial(kernel, nq, nl, cap, id_bytes), out_shap...  24.1 us
    pallas_call x1, Pallas kernels, hand_over(): pl.pallas_call(finish, out_shape=(jax.ShapeDtypeStruct(tv.shape, tv.dtype...  2.37 us

profile of v4, /device:TPU:0, one launch (start us, length us, event | category | flops | bytes accessed | tf_op | source)
XLA Modules:
  0.0 27.1 jit_solution(214603741296073125)
XLA Ops:
  0.6 24.1 %shard_map.86 = (bf16[256,768]{1,0:T(8,128)(2,1)}, f32[32,2,1,128]{3,2,1,0:T(1,128)}, s32[2,1,512]{2,1,0:T(1,128)}) custom-call(bf16[32,2048]{1,0:T(8,128)(2,1)} %qp_hbm.1, bf16[768,2048]{1,0:T(8,128)(2,1)} %lib_hbm.1, f32[8,192]{1,0:T(8,128)} %qa_hbm.1, f32[192,768]{1,0:T(8,128)} %bitcast.2, s32[8,64]{1,0:T(8,128)} %cand_hbm.1, s32[192,128]{1,0:T(8,128)} %bitcast.3), custom_call_target="tpu_custom_call" | custom-call | tf_op jit(solution)/shard_map/pallas_call | solution.py:487
  24.7 2.4 %shard_map.87 = (bf16[256,768]{1,0:T(8,128)(2,1)}, f32[8,64]{1,0:T(8,128)}) custom-call(bf16[256,768]{1,0:T(8,128)(2,1)} %get-tuple-element.5.tv_in, f32[32,2,1,128]{3,2,1,0:T(1,128)} %get-tuple-element.6.ret_in, s32[2,1,512]{2,1,0:T(1,128)} %get-tuple-element.7.meta, s32[8]{0:T(128)} %count.1), custom_call_target="tpu_custom_call" | custom-call | tf_op jit(solution)/shard_map/pallas_call | solution.py:462

commit v5 on v4

--- a/solution.py
+++ b/solution.py
@@ -92,10 +92,10 @@
 
 def kernel(
     nq, nl, cap, id_bytes,
-    qp_hbm, lib_hbm, qa_hbm, conf_hbm, cand_hbm, home_hbm,
+    qp_hbm, lib_hbm, qa_hbm, conf_hbm, cand_hbm, count_hbm, home_hbm,
     tv_hbm, ret_in, meta_hbm,
     tv_ref,
-    qp_ref, qa_ref, cand_ref, home_ref,
+    qp_ref, qa_ref, cand_ref, count_ref, home_ref,
     lib, turned, conf, gath, pack, atoms_in, codes_out, codes_in, score, meta,
     confp, ownprep, pairs_c, pairs_q, inv_ref, onehot, qonehot, cself, shape_s,
     loc_sem, s1_send, s1_recv, sib_send, sib_recv, s2_send, s2_recv,
@@ -137,7 +137,7 @@
     loads = [
         pltpu.make_async_copy(src, dst, loc_sem.at[2 + n])
         for n, (src, dst) in enumerate(
-            ((qa_hbm, qa_ref), (cand_hbm, cand_ref), (home_hbm, home_ref), (qp_hbm, qp_ref))
+            ((qa_hbm, qa_ref), (cand_hbm, cand_ref), (home_hbm, home_ref), (qp_hbm, qp_ref), (count_hbm, count_ref))
         )
     ]
     for load in loads:
@@ -221,7 +221,7 @@
         gath[k, pl.ds(pl.multiple_of(q * block, block), block), :] = qp_ref[:, k * cols : (k + 1) * cols]
     atoms_in[l, c, z] = pack[...]
 
-    for load in loads[1:3]:
+    for load in loads[1:3] + loads[4:]:
         load.wait()
 
     ids = jnp.concatenate([cand_ref[pl.ds(i, 1), :] for i in range(local_q)], axis=1)
@@ -246,9 +246,12 @@
     before = nn(owns_b, tri)
     rank = jnp.sum(jnp.where(owns, before, 0.0), axis=0, keepdims=True).astype(I32)
     my_off = lax.rem(cap * me, LANES)
-    meta[0] = owner
+    live = jnp.concatenate(
+        [jnp.where(iota((1, listed), 1) < count_ref[i], 1, 0) for i in range(local_q)], axis=1
+    )
+    meta[0] = jnp.where(live > 0, owner, -1)
     meta[1] = rank + my_off
-    meta_copy = pltpu.make_async_copy(meta, meta_hbm, loc_sem.at[6])
+    meta_copy = pltpu.make_async_copy(meta, meta_hbm, loc_sem.at[8])
     meta_copy.start()
     rank_b = jnp.where(iota((2 * LANES, cand_n), 0) == rank + my_off, 1.0, 0.0).astype(BF16)
     code = slot * local_q + fdiv(iota((1, cand_n), 1), listed) + 1
@@ -400,11 +403,10 @@
     take(part_prints, sib_recv.at[1])
     for r in range(0, rows, chunk):
         at = slice(r, r + chunk)
-        scores = None
-        for k in range(nl):
-            prod = nn(gath[k, at, :], turned[k * cols : (k + 1) * cols, :])
-            scores = prod if scores is None else scores + prod
-        tv_ref[at, :] = (scores * inv_ref[at, :]).astype(BF16)
+        part = jnp.concatenate([gath[k, at, :] for k in range(nl)], axis=1)
+        for n in range(0, own_rows, 2 * LANES):
+            wide = slice(n, n + 2 * LANES)
+            tv_ref[at, wide] = (nn(part, turned[:, wide]) * inv_ref[at, :]).astype(BF16)
 
     tv_copy = pltpu.make_async_copy(tv_ref, tv_hbm, loc_sem.at[7])
     tv_copy.start()
@@ -421,7 +423,7 @@
     for tq, tl in peers:
         at = lax.div(cap * (tq * nl + tl), LANES)
         remote(score.at[pl.ds(at, 2)], ret_in.at[me_o], send_d, recv_d, tq, tl).start()
-    own_copy = pltpu.make_async_copy(score.at[pl.ds(lax.div(cap * me, LANES), 2)], ret_in.at[me_o], loc_sem.at[5])
+    own_copy = pltpu.make_async_copy(score.at[pl.ds(lax.div(cap * me, LANES), 2)], ret_in.at[me_o], loc_sem.at[1])
     own_copy.start()
 
     take(gath.at[0, pl.ds(0, (nz - 1) * block), :], s1_send)
@@ -438,8 +440,8 @@
     take(ret_in.at[d_rest], send_d)
 
 
-def finish(tv_in, ret_in, meta, count, tv_out, out_ref, sem):
-    copy = pltpu.make_async_copy(tv_in, tv_out, sem)
+def finish(tv_in, ret_in, meta, tv_out, out_hbm, out_ref, sems):
+    copy = pltpu.make_async_copy(tv_in, tv_out, sems.at[0])
     copy.start()
     dev = ret_in.shape[0]
     local_q, listed = out_ref.shape
@@ -448,24 +450,25 @@
     rank_b = jnp.where(iota((2 * LANES, cand_n), 0) == meta[1], 1.0, 0.0).astype(BF16)
     came = jnp.concatenate([ret_in[:, k].reshape(dev, LANES) for k in range(2)], axis=1)
     hi_b, lo_b = split2(came)
-    mine = nn(hi_b, rank_b) + nn(lo_b, rank_b)
-    final = jnp.sum(jnp.where(owns, mine, 0.0), axis=0, keepdims=True)
+    mine = nn(jnp.concatenate([hi_b, lo_b], axis=0), rank_b)
+    final = jnp.sum(jnp.where(owns, mine[:dev] + mine[dev:], 0.0), axis=0, keepdims=True)
     for i in range(local_q):
-        line = final[:, i * listed : (i + 1) * listed]
-        live = iota((1, listed), 1) < count[i]
-        out_ref[i : i + 1, :] = jnp.where(live, line, 0.0)
+        out_ref[i : i + 1, :] = final[:, i * listed : (i + 1) * listed]
+    last = pltpu.make_async_copy(out_ref, out_hbm, sems.at[1])
+    last.start()
+    last.wait()
     copy.wait()
 
 
-def hand_over(tv, ret, meta, count, out_shape):
+def hand_over(tv, ret, meta, out_shape):
     vspec = pl.BlockSpec(memory_space=pltpu.VMEM)
     return pl.pallas_call(
         finish,
         out_shape=(jax.ShapeDtypeStruct(tv.shape, tv.dtype), jax.ShapeDtypeStruct(out_shape, F32)),
-        in_specs=[vspec, vspec, vspec, pl.BlockSpec(memory_space=pltpu.SMEM)],
-        out_specs=(pl.BlockSpec(memory_space=pl.ANY), vspec),
-        scratch_shapes=[pltpu.SemaphoreType.DMA],
-    )(tv, ret, meta, count)
+        in_specs=[vspec] * 3,
+        out_specs=(pl.BlockSpec(memory_space=pl.ANY), pl.BlockSpec(memory_space=pl.ANY)),
+        scratch_shapes=[pltpu.VMEM(out_shape, F32), pltpu.SemaphoreType.DMA((2,))],
+    )(tv, ret, meta)
 
 
 def body(nq, nl, query_prints, library_prints, query_atoms, conformer_atoms, candidates, candidate_count, home_row):
@@ -491,13 +494,14 @@
             jax.ShapeDtypeStruct((dev, 2, 1, LANES), F32),
             jax.ShapeDtypeStruct((2, 1, cand_n), I32),
         ),
-        in_specs=[pl.BlockSpec(memory_space=pltpu.HBM)] * 6,
+        in_specs=[pl.BlockSpec(memory_space=pltpu.HBM)] * 7,
         out_specs=(hspec, hspec, hspec),
         scratch_shapes=[
             vm((rows, own_rows), BF16),
             vm((block, width), BF16),
             vm((local_q, 4 * atoms), F32),
             vm((local_q, listed), I32),
+            pltpu.SMEM((local_q,), I32),
             vm((home_row.shape[0] // LANES, LANES), I32),
             vm((own_rows, width), BF16),
             vm((width, own_rows), BF16),
@@ -518,7 +522,7 @@
             vm((rows, pairs), BF16),
             vm((1, own_rows), F32),
             vm((1, pairs), F32),
-            dma((8,)),
+            dma((9,)),
             dma, dma((nz,)),
             dma, dma((2,)),
             dma, dma((nz, nl)),
@@ -529,10 +533,10 @@
             collective_id=0, has_side_effects=True, vmem_limit_bytes=limit
         ),
     )(
-        query_prints, library_prints, query_atoms, conformer_atoms.T, candidates,
+        query_prints, library_prints, query_atoms, conformer_atoms.T, candidates, candidate_count,
         home_row.reshape(-1, LANES),
     )
-    return hand_over(tv, ret, meta, candidate_count, (local_q, listed))
+    return hand_over(tv, ret, meta, (local_q, listed))
 
 
 def solution(mesh):

time: 27.3 us -> 26.8 us (0.982)
  Pallas kernels: 26.5 us -> 26 us
    pallas_call x1, Pallas kernels: 2.37 us -> 1.9 us  [hand_over(): pl.pallas_call(finish, out_shape=(jax.ShapeDtypeStruct(tv.shape, tv.dtype...]
where the time goes in v5:
time: 26.8 us; the launch traced here: 26.6 us
  Pallas kernels  26 us (97%)
  between operations  0.64 us (2%)
    pallas_call x1, Pallas kernels, body(): pl.pallas_call(functools.partial(kernel, nq, nl, cap, id_bytes), out_shap...  24.1 us
    pallas_call x1, Pallas kernels, hand_over(): pl.pallas_call(finish, out_shape=(jax.ShapeDtypeStruct(tv.shape, tv.dtype...  1.9 us

profile of v5, /device:TPU:0, one launch (start us, length us, event | category | flops | bytes accessed | tf_op | source)
XLA Modules:
  0.0 26.6 jit_solution(5025100664639748480)
XLA Ops:
  0.6 24.1 %shard_map.86 = (bf16[256,768]{1,0:T(8,128)(2,1)}, f32[32,2,1,128]{3,2,1,0:T(1,128)}, s32[2,1,512]{2,1,0:T(1,128)}) custom-call(bf16[32,2048]{1,0:T(8,128)(2,1)} %qp_hbm.1, bf16[768,2048]{1,0:T(8,128)(2,1)} %lib_hbm.1, f32[8,192]{1,0:T(8,128)} %qa_hbm.1, f32[192,768]{1,0:T(8,128)} %bitcast.2, s32[8,64]{1,0:T(8,128)} %cand_hbm.1, s32[8]{0:T(128)} %count_hbm.1, ...), custom_call_target="tpu_custom_call" | custom-call | tf_op jit(solution)/shard_map/pallas_call | solution.py:490
  24.7 1.9 %shard_map.87 = (bf16[256,768]{1,0:T(8,128)(2,1)}, f32[8,64]{1,0:T(8,128)}) custom-call(bf16[256,768]{1,0:T(8,128)(2,1)} %get-tuple-element.5.tv_in, f32[32,2,1,128]{3,2,1,0:T(1,128)} %get-tuple-element.6.ret_in, s32[2,1,512]{2,1,0:T(1,128)} %get-tuple-element.7.meta), custom_call_target="tpu_custom_call" | custom-call | tf_op jit(solution)/shard_map/pallas_call | solution.py:465
